TPU v7x, 512 devices: a whole 4x4x16 slice. The times are simulated.
512 devices in a mesh: seq: 64 (over x_hi, z, core), head: 8 (over x_lo, y).
Axes of the slice: x: 4 (x_hi: 2, x_lo: 2; x = x_hi * 2 + x_lo), y: 4, z: 16, core: 2. Of those that a mesh axis runs over, the one named last changes fastest.
Arguments:
- queries: bfloat16 [32768, 4096], P(('seq', 'head')), may hold values from -5 to 5
- keys: bfloat16 [32768, 1024], P(('seq', 'head')), may hold values from -5 to 5
- values: bfloat16 [32768, 1024], P(('seq', 'head')), may hold values from -5 to 5
- upstream: bfloat16 [32768, 4096], P('seq', 'head'), may hold values from -786432 to 786432
- loss_mask: int32 [32768], P('seq'), may hold values 0 or 1
- parents: int32 [64], replicated, may hold values from -1 to 62, as said below
- token_count: int32 [1], replicated, may hold values from 8192 to 32768
Outputs:
- attended: bfloat16 [32768, 4096], P('seq', 'head')
- query_gradient: bfloat16 [32768, 4096], P('seq', 'head')
- key_gradient: bfloat16 [32768, 1024], P('seq', 'head')
- value_gradient: bfloat16 [32768, 1024], P('seq', 'head')
Inputs may be any that keep to these rules, and one draw needn't show every extreme that they name: A rollout tree is a run of at most 3 consecutive segments; parents[g] is -1 for its first segment and otherwise an earlier segment of the same tree, so every ancestor of g lies at most 2 segments before g. In every draw the first 3 segments form one chain, each the child of the one before, and so do the last 3.
All inputs are finite; a program needn't handle non-finite values. No bound on the sum of `loss_mask` on one device may be relied on, other than what follows from the above.
Results may differ from a plain program's by a relative error of at most 0.028.
Values may be sent and summed in bfloat16 or wider, within the bound.
A program may use at most 64 MiB of HBM per device.

v0:
```python
import math

import jax
import jax.numpy as jnp
from jax import lax
from jax.sharding import PartitionSpec as P

QUERY_HEAD_COUNT = 32
KEY_VALUE_HEADS = 8
HEAD_SIZE = 128
ANCESTOR_SPAN = 2


def from_behind(array, axis, by):
    size = lax.axis_size(axis)
    pairs = [(i, i + by) for i in range(size) if 0 <= i + by < size]
    return lax.ppermute(array, axis, pairs)


def table_entry(table, position):
    slot_ids = jnp.arange(table.shape[0], dtype=jnp.int32)
    return jnp.sum(jnp.where(slot_ids == position, table, 0))


def ancestor_gates(parents, segment):
    current = table_entry(parents, segment)
    ancestry = [jnp.zeros((), jnp.bool_) for segment_gap in range(ANCESTOR_SPAN)]
    for walk_step in range(ANCESTOR_SPAN):
        for segment_gap in range(1, ANCESTOR_SPAN + 1):
            ancestry[segment_gap - 1] = ancestry[segment_gap - 1] | (current >= 0) & (
                current == segment - segment_gap
            )
        current = jnp.where(current >= 0, table_entry(parents, current), -1)
    return ancestry


def tile_scores(query_heads, key_block, allowed, score_scale):
    key_heads = key_block.reshape(key_block.shape[0], -1, query_heads.shape[-1])
    scores = (
        jnp.einsum("tkgd,skd->kgts", query_heads, key_heads, preferred_element_type=jnp.float32)
        * score_scale
    )
    return jnp.where(allowed, scores, -jnp.inf)


def per_device(queries, keys, values, upstream, loss_mask, parents, token_count):
    local_queries, local_keys, local_values = (
        lax.all_to_all(queries, "head", split_axis=1, concat_axis=0, tiled=True),
        lax.all_to_all(keys, "head", split_axis=1, concat_axis=0, tiled=True),
        lax.all_to_all(values, "head", split_axis=1, concat_axis=0, tiled=True),
    )
    tok_rows = local_queries.shape[0]
    local_groups = local_keys.shape[1] // HEAD_SIZE
    query_head_group = QUERY_HEAD_COUNT // KEY_VALUE_HEADS
    score_scale = 1.0 / math.sqrt(HEAD_SIZE)
    query_heads = local_queries.reshape(tok_rows, local_groups, query_head_group, HEAD_SIZE)
    segment = lax.axis_index("seq")
    ancestry = ancestor_gates(parents, segment)
    remote_kv = []
    for segment_gap in range(1, ANCESTOR_SPAN + 1):
        remote_kv.append(from_behind((local_keys, local_values), "seq", segment_gap))
    positions = jnp.arange(tok_rows, dtype=jnp.int32)
    causal = positions[:, None] >= positions[None, :]
    own_scores = tile_scores(query_heads, local_keys, causal, score_scale)
    row_max = jnp.max(own_scores, axis=-1)
    row_total = jnp.sum(jnp.exp(own_scores - row_max[..., None]), axis=-1)
    for segment_gap in range(ANCESTOR_SPAN):

        def merge_stats(
            running, key_block=remote_kv[segment_gap][0], gate_flag=ancestry[segment_gap]
        ):
            old_max, old_total = running
            scores = tile_scores(query_heads, key_block, gate_flag, score_scale)
            new_max = jnp.maximum(old_max, jnp.max(scores, axis=-1))
            new_total = old_total * jnp.exp(old_max - new_max) + jnp.sum(
                jnp.exp(scores - new_max[..., None]), axis=-1
            )
            return (new_max, new_total)

        row_max, row_total = merge_stats((row_max, row_total))
    lse = row_max + jnp.log(row_total)

    def tile_probs(key_block, allowed):
        return jnp.exp(
            tile_scores(query_heads, key_block, allowed, score_scale) - lse[..., None]
        ).astype(jnp.bfloat16)

    def value_heads(value_block):
        return value_block.reshape(tok_rows, local_groups, HEAD_SIZE)

    own_probs = tile_probs(local_keys, causal)
    out_total = jnp.einsum(
        "kgts,skd->tkgd", own_probs, value_heads(local_values), preferred_element_type=jnp.float32
    )
    for segment_gap in range(ANCESTOR_SPAN):

        def add_values(
            carried,
            key_block=remote_kv[segment_gap][0],
            value_block=remote_kv[segment_gap][1],
            gate_flag=ancestry[segment_gap],
        ):
            probs = tile_probs(key_block, gate_flag)
            return carried + jnp.einsum(
                "kgts,skd->tkgd",
                probs,
                value_heads(value_block),
                preferred_element_type=jnp.float32,
            )

        out_total = add_values(out_total)
    attended = out_total.astype(jnp.bfloat16)
    token_weight = loss_mask.astype(jnp.float32) / token_count[0].astype(jnp.float32)
    grad_out = (upstream.astype(jnp.float32) * token_weight[:, None]).astype(jnp.bfloat16)
    grad_heads = grad_out.reshape(tok_rows, local_groups, query_head_group, HEAD_SIZE)
    delta = jnp.sum(
        grad_heads.astype(jnp.float32) * attended.astype(jnp.float32), axis=-1
    ).transpose(1, 2, 0)

    def tile_grads(key_block, value_block, allowed):
        probs = tile_probs(key_block, allowed)
        key_heads = key_block.reshape(tok_rows, local_groups, HEAD_SIZE)
        dprob = jnp.einsum(
            "tkgd,skd->kgts",
            grad_heads,
            value_heads(value_block),
            preferred_element_type=jnp.float32,
        )
        dscore = (probs.astype(jnp.float32) * (dprob - delta[..., None])).astype(jnp.bfloat16)
        query_part = (
            jnp.einsum("kgts,skd->tkgd", dscore, key_heads, preferred_element_type=jnp.float32)
            * score_scale
        )
        key_part = (
            jnp.einsum("kgts,tkgd->skd", dscore, query_heads, preferred_element_type=jnp.float32)
            * score_scale
        )
        value_part = jnp.einsum(
            "kgts,tkgd->skd", probs, grad_heads, preferred_element_type=jnp.float32
        )
        return (query_part, key_part.reshape(tok_rows, -1), value_part.reshape(tok_rows, -1))

    query_total, own_key, own_value = tile_grads(local_keys, local_values, causal)
    returns = []
    for segment_gap in range(ANCESTOR_SPAN):

        def ancestor_tile(
            operand,
            key_block=remote_kv[segment_gap][0],
            value_block=remote_kv[segment_gap][1],
            gate_flag=ancestry[segment_gap],
        ):
            return tile_grads(key_block, value_block, gate_flag)

        query_part, key_part, value_part = ancestor_tile(0)
        query_total = query_total + query_part
        returns.append((key_part, value_part))
    key_back = own_key
    value_back = own_value
    for segment_gap in range(1, ANCESTOR_SPAN + 1):
        arrived = from_behind(
            (returns[segment_gap - 1][0], returns[segment_gap - 1][1]), "seq", -segment_gap
        )
        key_back = key_back + arrived[0]
        value_back = value_back + arrived[1]
    return (
        attended.reshape(tok_rows, -1),
        query_total.astype(jnp.bfloat16).reshape(tok_rows, -1),
        key_back.astype(jnp.bfloat16),
        value_back.astype(jnp.bfloat16),
    )


def solution(mesh):
    in_specs = (
        P(("seq", "head"), None),
        P(("seq", "head"), None),
        P(("seq", "head"), None),
        P("seq", "head"),
        P("seq"),
        P(),
        P(),
    )
    out_specs = (P("seq", "head"), P("seq", "head"), P("seq", "head"), P("seq", "head"))
    return jax.shard_map(
        per_device, mesh=mesh, in_specs=in_specs, out_specs=out_specs, check_vma=False
    )
```

profile of v0, /device:TPU:7, one launch (start us, length us, event | category | flops | bytes accessed | tf_op | source)
XLA Modules:
  0.0 102.5 jit_solution(10611363252690973126)
XLA Ops:
  0.6 0.9 copy-done
  1.5 0.7 copy_bitcast_fusion.2
  2.2 5.4 %all-to-all-start = ((bf16[64,8,128]{2,0,1:T(8,128)(2,1)}), bf16[64,8,128]{2,0,1:T(8,128)(2,1)S(1)}, u32[]{:S(2)}, u32[]{:S(2)}) async-start(bf16[64,8,128]{2,0,1:T(8,128)(2,1)} %copy_bitcast_fusion.2), calls=%async_computation | async-start | bytes 262144 | tf_op jit(solution)/shard_map/all_to_all | solution.py:49
  7.6 1.6 %copy_bitcast_fusion.1 = bf16[64,8,128]{2,0,1:T(8,128)(2,1)} fusion(bf16[64,1024]{1,0:T(8,128)(2,1)} %param.9), kind=kLoop, calls=%fused_computation.88 | loop fusion | bytes 262144 | tf_op jit(solution)/shard_map/all_to_all | solution.py:50
  9.2 1.9 %copy.206 = bf16[8,8,8,512]{3,2,0,1:T(8,128)(2,1)} copy(bf16[8,8,8,512]{3,2,1,0:T(8,128)(2,1)} %bitcast.296) | data formatting | bytes 1048576 | tf_op jit(solution)/shard_map/all_to_all | solution.py:48
  11.7 1.3 %fusion.122 = s32[]{:T(128)} fusion(s32[64]{0:T(128)} %param.12, s32[]{:T(128)S(6)} %axis_index.15), kind=kLoop, calls=%fused_computation.102 | loop fusion | flops 191 | bytes 264 | tf_op jit(solution)/shard_map/reduce_sum | solution.py:22
  13.6 5.2 %all-to-all-start.2 = ((bf16[64,8,128]{2,0,1:T(8,128)(2,1)}), bf16[64,8,128]{2,0,1:T(8,128)(2,1)S(1)}, u32[]{:S(2)}, u32[]{:S(2)}) async-start(bf16[64,8,128]{2,0,1:T(8,128)(2,1)} %copy_bitcast_fusion.1), calls=%async_computation.2 | async-start | bytes 262144 | tf_op jit(solution)/shard_map/all_to_all | solution.py:50
  18.7 0.7 convert_divide_fusion
  19.4 3.7 %all-to-all-done.2 = bf16[64,8,128]{2,0,1:T(8,128)(2,1)S(1)} async-done(((bf16[64,8,128]{2,0,1:T(8,128)(2,1)}), bf16[64,8,128]{2,0,1:T(8,128)(2,1)S(1)}, u32[]{:S(2)}, u32[]{:S(2)}) %all-to-all-start.2) | async-done | bytes 131104 | tf_op jit(solution)/shard_map/all_to_all | solution.py:50
  23.1 4.5 %all-to-all-start.1 = ((bf16[64,8,512]{2,0,1:T(8,128)(2,1)}), bf16[64,8,512]{2,0,1:T(8,128)(2,1)S(1)}, u32[]{:S(2)}, u32[]{:S(2)}) async-start(bf16[64,8,512]{2,0,1:T(8,128)(2,1)} %bitcast.278), calls=%async_computation.1 | async-start | bytes 1048576 | tf_op jit(solution)/shard_map/all_to_all | solution.py:48
  27.6 1.9 %fusion.123 = s32[]{:T(128)} fusion(s32[64]{0:T(128)} %param.12, s32[]{:T(128)} %fusion.122), kind=kLoop, calls=%fused_computation.103 | loop fusion | flops 191 | bytes 264 | tf_op jit(solution)/shard_map/reduce_sum | solution.py:22
  31.2 1.2 %multiply_convert_fusion = bf16[512,512]{1,0:T(8,128)(2,1)S(1)} fusion(bf16[512,512]{1,0:T(8,128)(2,1)} %param.10, f32[512]{0:T(512)S(1)} %convert_divide_fusion), kind=kLoop, calls=%fused_computation.76 | loop fusion | flops 786432 | bytes 1050624 | tf_op jit(solution)/shard_map/convert_element_type | solution.py:114
  32.4 0.2 copy.181
  32.7 1.2 %copy.132 = f32[512,512]{0,1:T(8,128)} copy(bf16[512,512]{1,0:T(8,128)(2,1)S(1)} %multiply_convert_fusion) | data formatting | bytes 1572864 | tf_op jit(solution)/shard_map/convert_element_type | solution.py:117
  33.9 3.5 %collective-permute-start.1 = (bf16[512,128]{1,0:T(8,128)(2,1)S(1)}, bf16[512,128]{1,0:T(8,128)(2,1)S(1)}, u32[]{:S(2)}, u32[]{:S(2)}) collective-permute-start(bf16[512,128]{1,0:T(8,128)(2,1)S(1)} %bitcast.292), channel_id=1, source_target_pairs={{0,16},{8,24},{16,32},{24,40},{32,48},{40,56},{48,64},{56,72},{64,... | collective-permute-start | bytes 393224 | tf_op jit(solution)/shard_map/ppermute | solution.py:17
  37.5 6.7 %collective-permute-start = (bf16[512,128]{1,0:T(8,128)(2,1)S(1)}, bf16[512,128]{1,0:T(8,128)(2,1)S(1)}, u32[]{:S(2)}, u32[]{:S(2)}) collective-permute-start(bf16[512,128]{1,0:T(8,128)(2,1)S(1)} %bitcast.293), channel_id=1, source_target_pairs={{0,8},{8,16},{16,24},{24,32},{32,40},{40,48},{48,56},{56,64},{64,7... | collective-permute-start | bytes 393224 | tf_op jit(solution)/shard_map/ppermute | solution.py:17
  44.1 0.8 copy.126
  44.9 3.5 %collective-permute-start.3 = (bf16[512,128]{0,1:T(8,128)(2,1)}, bf16[512,128]{0,1:T(8,128)(2,1)}, u32[]{:S(2)}, u32[]{:S(2)}) collective-permute-start(bf16[512,128]{0,1:T(8,128)(2,1)} %copy.126), channel_id=1, source_target_pairs={{0,16},{8,24},{16,32},{24,40},{32,48},{40,56},{48,64},{56,72},{64,... | collective-permute-start | bytes 393224 | tf_op jit(solution)/shard_map/ppermute | solution.py:17
  48.5 2.2 %collective-permute-start.2 = (bf16[512,128]{0,1:T(8,128)(2,1)}, bf16[512,128]{0,1:T(8,128)(2,1)}, u32[]{:S(2)}, u32[]{:S(2)}) collective-permute-start(bf16[512,128]{0,1:T(8,128)(2,1)} %copy.126), channel_id=1, source_target_pairs={{0,8},{8,16},{16,24},{24,32},{32,40},{40,48},{48,56},{56,64},{64,7... | collective-permute-start | bytes 393224 | tf_op jit(solution)/shard_map/ppermute | solution.py:17
  50.8 0.9 fusion.14
  51.7 0.9 exponential_reduce_fusion
  52.7 0.7 bitcast_reduce_fusion
  53.4 0.7 bitcast_reduce_fusion.1
  54.2 1.7 %fusion.7 = (f32[4,512]{1,0:T(4,128)S(1)}, f32[4,512]{1,0:T(4,128)S(1)}) fusion(f32[512,512,4]{1,0,2:T(8,128)S(1)} %get-tuple-element.26, f32[4,512]{1,0:T(4,128)S(1)} %get-tuple-element.20, pred[]{:T(512)S(6)} %or.7, f32[4,512]{1,0:T(4,128)S(1)} %get-tuple-element.21, f32[512,512,4]{1,0,2:T(8,128)S(1)} %get-tuple-element.30, pred[]{:T(512)S(6)} %or.6), kind=kLoop, calls=%fused_computation.14 | loop fusion | flops 8384512 | bytes 8421378 | tf_op jit(solution)/shard_map/reduce_sum | solution.py:75
  55.9 2.6 %fusion.13 = (bf16[1,4,512,512]{2,3,1,0:T(8,128)(2,1)S(1)}, bf16[1,4,512,512]{2,3,1,0:T(8,128)(2,1)S(1)}, bf16[1,4,512,512]{2,3,1,0:T(8,128)(2,1)S(1)}) fusion(f32[512,512,4]{1,0,2:T(8,128)S(1)} %get-tuple-element.30, f32[4,512]{1,0:T(4,128)S(1)} %log_add_fusion, pred[]{:T(512)S(6)} %or.6, f32[512,512,4]{1,0,2:T(8,128)S(1)} %get-tuple-element.26, ...), kind=kLoop, calls=%fused_computation.23 | loop fusion | flops 12582912 | bytes 19144706 | tf_op jit(solution)/shard_map/convert_element_type | solution.py:86
  58.5 1.5 %fusion.63 = f32[512,128]{0,1:T(8,128)} fusion(bf16[512,4,128]{0,2,1:T(8,128)(2,1)S(1)} %bitcast.279, bf16[1,4,512,512]{2,3,1,0:T(8,128)(2,1)S(1)} %get-tuple-element.22), kind=kOutput, calls=%fused_computation.61 | convolution fusion | flops 268435456 | bytes 2883584 | tf_op jit(solution)/shard_map/kgts,tkgd->skd/dot_general | solution.py:138
  60.0 2.1 %collective-permute-start.6 = (f32[512,128]{0,1:T(8,128)}, f32[512,128]{0,1:T(8,128)S(1)}, u32[]{:S(2)}, u32[]{:S(2)}) collective-permute-start(f32[512,128]{0,1:T(8,128)} %fusion.63), channel_id=1, source_target_pairs={{8,0},{16,8},{24,16},{32,24},{40,32},{48,40},{56,48},{64,56},{72,6... | collective-permute-start | bytes 786440 | tf_op jit(solution)/shard_map/ppermute | solution.py:17
  62.1 1.5 %fusion.66 = f32[512,128]{0,1:T(8,128)} fusion(bf16[512,4,128]{0,2,1:T(8,128)(2,1)S(1)} %bitcast.280, bf16[1,4,512,512]{2,3,1,0:T(8,128)(2,1)S(1)} %get-tuple-element.23), kind=kOutput, calls=%fused_computation.62 | convolution fusion | flops 268435456 | bytes 2883584 | tf_op jit(solution)/shard_map/kgts,tkgd->skd/dot_general | solution.py:138
  63.6 6.6 %collective-permute-start.7 = (f32[512,128]{0,1:T(8,128)}, f32[512,128]{0,1:T(8,128)}, u32[]{:S(2)}, u32[]{:S(2)}) collective-permute-start(f32[512,128]{0,1:T(8,128)} %fusion.66), channel_id=1, source_target_pairs={{16,0},{24,8},{32,16},{40,24},{48,32},{56,40},{64,48},{72,56},{80,... | collective-permute-start | bytes 786440 | tf_op jit(solution)/shard_map/ppermute | solution.py:17
  70.2 0.5 fusion.37
  70.7 1.4 %fusion.29 = f32[4,512,128]{1,2,0:T(8,128)S(1)} fusion(bf16[1,4,512,512]{2,3,1,0:T(8,128)(2,1)S(1)} %get-tuple-element.23, bf16[512,128]{0,1:T(8,128)(2,1)} %collective-permute-done.3), kind=kOutput, calls=%fused_computation.43 | convolution fusion | flops 268435456 | bytes 3276800 | tf_op jit(solution)/shard_map/kgts,skd->tkgd/dot_general | solution.py:104
  72.1 2.3 %multiply_reduce_fusion = (f32[512,4]{0,1:T(4,128)S(1)}, bf16[4,512,128]{1,2,0:T(8,128)(2,1)}) fusion(f32[512,1,4,128]{0,3,2,1:T(8,128)S(1)} %bitcast.285, f32[4,512,128]{1,2,0:T(8,128)S(1)} %fusion.29, f32[4,512,128]{1,2,0:T(8,128)S(1)} %fusion.37, bf16[1,4,512,512]{2,3,1,0:T(8,128)(2,1)S(1)} %get-tuple-element.22, bf16[512,128]{0,1:T(8,128)(2,1)} %collective-permute-done.2), kind=kOutput, calls=%fused_computation.75 | convolution fusion | flops 270006272 | bytes 5906432 | tf_op jit(solution)/shard_map/kgts,skd->tkgd/dot_general | solution.py:104
  74.4 0.7 fusion.5
  75.1 2.1 %fusion.3 = bf16[1,4,512,512]{2,3,1,0:T(8,128)(2,1)S(1)} fusion(bf16[1,4,512,512]{2,3,1,0:T(8,128)(2,1)S(1)} %get-tuple-element.22, bf16[512,4,128]{0,2,1:T(8,128)(2,1)S(1)} %bitcast.282, f32[4,512]{1,0:T(4,128)S(1)} %bitcast.298, bf16[512,128]{0,1:T(8,128)(2,1)} %collective-permute-done.2), kind=kOutput, calls=%fused_computation.5 | convolution fusion | flops 272629760 | bytes 4857856 | tf_op jit(solution)/shard_map/tkgd,skd->kgts/dot_general | solution.py:123
  77.2 1.4 %fusion.81 = f32[512,128]{1,0:T(8,128)} fusion(bf16[1,4,512,512]{2,3,1,0:T(8,128)(2,1)S(1)} %fusion.3, bf16[512,4,128]{2,1,0:T(4,128)(2,1)S(1)} %reshape.287), kind=kOutput, calls=%fused_computation.67 | convolution fusion | flops 268500992 | bytes 2883584 | tf_op jit(solution)/shard_map/kgts,tkgd->skd/dot_general | solution.py:135
  78.6 4.0 %collective-permute-start.4 = (f32[512,128]{1,0:T(8,128)}, f32[512,128]{1,0:T(8,128)}, u32[]{:S(2)}, u32[]{:S(2)}) collective-permute-start(f32[512,128]{1,0:T(8,128)} %fusion.81), channel_id=1, source_target_pairs={{8,0},{16,8},{24,16},{32,24},{40,32},{48,40},{56,48},{64,56},{72,6... | collective-permute-start | bytes 786440 | tf_op jit(solution)/shard_map/ppermute | solution.py:17
  82.6 1.9 %fusion.1 = bf16[1,4,512,512]{2,3,1,0:T(8,128)(2,1)S(1)} fusion(bf16[1,4,512,512]{2,3,1,0:T(8,128)(2,1)S(1)} %get-tuple-element.23, bf16[512,4,128]{0,2,1:T(8,128)(2,1)S(1)} %bitcast.283, f32[4,512]{1,0:T(4,128)S(1)} %bitcast.299, bf16[512,128]{0,1:T(8,128)(2,1)} %collective-permute-done.3), kind=kOutput, calls=%fused_computation.2 | convolution fusion | flops 272629760 | bytes 4857856 | tf_op jit(solution)/shard_map/tkgd,skd->kgts/dot_general | solution.py:123
  84.6 1.4 %fusion.78 = f32[512,128]{1,0:T(8,128)} fusion(bf16[1,4,512,512]{2,3,1,0:T(8,128)(2,1)S(1)} %fusion.1, bf16[512,4,128]{2,1,0:T(4,128)(2,1)S(1)} %reshape.287), kind=kOutput, calls=%fused_computation.66 | convolution fusion | flops 268500992 | bytes 2883584 | tf_op jit(solution)/shard_map/kgts,tkgd->skd/dot_general | solution.py:135
  86.0 3.6 %collective-permute-start.5 = (f32[512,128]{1,0:T(8,128)}, f32[512,128]{1,0:T(8,128)}, u32[]{:S(2)}, u32[]{:S(2)}) collective-permute-start(f32[512,128]{1,0:T(8,128)} %fusion.78), channel_id=1, source_target_pairs={{16,0},{24,8},{32,16},{40,24},{48,32},{56,40},{64,48},{72,56},{80,... | collective-permute-start | bytes 786440 | tf_op jit(solution)/shard_map/ppermute | solution.py:17
  89.6 0.5 fusion.25
  90.1 0.5 fusion.17
  90.6 1.4 %fusion.57 = bf16[4,512,128]{1,2,0:T(8,128)(2,1)} fusion(f32[4,512,128]{1,2,0:T(8,128)S(1)} %fusion.17, f32[4,512,128]{1,2,0:T(8,128)S(1)} %fusion.25, bf16[1,4,512,512]{2,3,1,0:T(8,128)(2,1)S(1)} %fusion.3, bf16[512,128]{1,0:T(8,128)(2,1)S(1)} %copy-done.10), kind=kOutput, calls=%fused_computation.59 | convolution fusion | flops 269484032 | bytes 4849664 | tf_op jit(solution)/shard_map/kgts,skd->tkgd/dot_general | solution.py:131
  92.1 2.0 %copy.155 = bf16[512,512]{1,0:T(8,128)(2,1)} copy(bf16[512,512]{0,1:T(8,128)(2,1)} %bitcast.287) | data formatting | bytes 1048576
  94.1 2.0 %copy.154 = bf16[512,512]{1,0:T(8,128)(2,1)} copy(bf16[512,512]{0,1:T(8,128)(2,1)} %bitcast.286) | data formatting | bytes 1048576
  96.2 0.7 copy-done.11
  96.8 1.8 %fusion.99 = bf16[512,128]{0,1:T(8,128)(2,1)S(1)} fusion(f32[512,128]{0,1:T(8,128)} %collective-permute-done.7, f32[512,128]{0,1:T(8,128)} %copy-done.11, bf16[512,4,128]{0,2,1:T(8,128)(2,1)S(1)} %bitcast.284, bf16[1,4,512,512]{2,3,1,0:T(8,128)(2,1)S(1)} %get-tuple-element.24), kind=kOutput, calls=%fused_computation.73 | convolution fusion | flops 268632064 | bytes 3276800 | tf_op jit(solution)/shard_map/kgts,tkgd->skd/dot_general | solution.py:138
  98.7 0.8 copy.156
  99.4 3.1 %fusion.102 = bf16[512,128]{1,0:T(8,128)(2,1)} fusion(f32[512,128]{1,0:T(8,128)} %collective-permute-done.5, f32[512,128]{1,0:T(8,128)} %collective-permute-done.4, bf16[1,4,512,512]{2,3,1,0:T(8,128)(2,1)} %copy-done.1, bf16[512,4,128]{2,1,0:T(4,128)(2,1)S(1)} %reshape.287), kind=kOutput, calls=%fused_computation.74 | convolution fusion | flops 268697600 | bytes 3276800 | tf_op jit(solution)/shard_map/kgts,tkgd->skd/dot_general | solution.py:135
  (36 shorter events, 0.3 us)
Async XLA Ops:
  0.6 0.9 copy-start
  2.2 11.3 %all-to-all-start = ((bf16[64,8,128]{2,0,1:T(8,128)(2,1)}), bf16[64,8,128]{2,0,1:T(8,128)(2,1)S(1)}, u32[]{:S(2)}, u32[]{:S(2)}) async-start(bf16[64,8,128]{2,0,1:T(8,128)(2,1)} %copy_bitcast_fusion.2), calls=%async_computation | async-start | bytes 262144 | tf_op jit(solution)/shard_map/all_to_all | solution.py:49
  13.6 38.1 %copy-start.5 = (bf16[64,8,128]{2,0,1:T(8,128)(2,1)}, bf16[64,8,128]{2,0,1:T(8,128)(2,1)S(1)}, u32[]{:S(2)}) copy-start(bf16[64,8,128]{2,0,1:T(8,128)(2,1)S(1)} %all-to-all-done) | copy-start | bytes 393220
  13.6 9.5 %all-to-all-start.2 = ((bf16[64,8,128]{2,0,1:T(8,128)(2,1)}), bf16[64,8,128]{2,0,1:T(8,128)(2,1)S(1)}, u32[]{:S(2)}, u32[]{:S(2)}) async-start(bf16[64,8,128]{2,0,1:T(8,128)(2,1)} %copy_bitcast_fusion.1), calls=%async_computation.2 | async-start | bytes 262144 | tf_op jit(solution)/shard_map/all_to_all | solution.py:50
  23.1 28.6 %copy-start.3 = (bf16[64,8,128]{2,0,1:T(8,128)(2,1)}, bf16[64,8,128]{2,0,1:T(8,128)(2,1)S(1)}, u32[]{:S(2)}) copy-start(bf16[64,8,128]{2,0,1:T(8,128)(2,1)S(1)} %all-to-all-done.2) | copy-start | bytes 393220
  23.1 27.6 %all-to-all-start.1 = ((bf16[64,8,512]{2,0,1:T(8,128)(2,1)}), bf16[64,8,512]{2,0,1:T(8,128)(2,1)S(1)}, u32[]{:S(2)}, u32[]{:S(2)}) async-start(bf16[64,8,512]{2,0,1:T(8,128)(2,1)} %bitcast.278), calls=%async_computation.1 | async-start | bytes 1048576 | tf_op jit(solution)/shard_map/all_to_all | solution.py:48
  33.9 18.7 %collective-permute-start.1 = (bf16[512,128]{1,0:T(8,128)(2,1)S(1)}, bf16[512,128]{1,0:T(8,128)(2,1)S(1)}, u32[]{:S(2)}, u32[]{:S(2)}) collective-permute-start(bf16[512,128]{1,0:T(8,128)(2,1)S(1)} %bitcast.292), channel_id=1, source_target_pairs={{0,16},{8,24},{16,32},{24,40},{32,48},{40,56},{48,64},{56,72},{64,... | collective-permute-start | bytes 393224 | tf_op jit(solution)/shard_map/ppermute | solution.py:17
  37.5 15.9 %collective-permute-start = (bf16[512,128]{1,0:T(8,128)(2,1)S(1)}, bf16[512,128]{1,0:T(8,128)(2,1)S(1)}, u32[]{:S(2)}, u32[]{:S(2)}) collective-permute-start(bf16[512,128]{1,0:T(8,128)(2,1)S(1)} %bitcast.293), channel_id=1, source_target_pairs={{0,8},{8,16},{16,24},{24,32},{32,40},{40,48},{48,56},{56,64},{64,7... | collective-permute-start | bytes 393224 | tf_op jit(solution)/shard_map/ppermute | solution.py:17
  44.9 25.8 %collective-permute-start.3 = (bf16[512,128]{0,1:T(8,128)(2,1)}, bf16[512,128]{0,1:T(8,128)(2,1)}, u32[]{:S(2)}, u32[]{:S(2)}) collective-permute-start(bf16[512,128]{0,1:T(8,128)(2,1)} %copy.126), channel_id=1, source_target_pairs={{0,16},{8,24},{16,32},{24,40},{32,48},{40,56},{48,64},{56,72},{64,... | collective-permute-start | bytes 393224 | tf_op jit(solution)/shard_map/ppermute | solution.py:17
  48.5 23.6 %collective-permute-start.2 = (bf16[512,128]{0,1:T(8,128)(2,1)}, bf16[512,128]{0,1:T(8,128)(2,1)}, u32[]{:S(2)}, u32[]{:S(2)}) collective-permute-start(bf16[512,128]{0,1:T(8,128)(2,1)} %copy.126), channel_id=1, source_target_pairs={{0,8},{8,16},{16,24},{24,32},{32,40},{40,48},{48,56},{56,64},{64,7... | collective-permute-start | bytes 393224 | tf_op jit(solution)/shard_map/ppermute | solution.py:17
  52.7 1.5 %copy-start.7 = (bf16[512,128]{1,0:T(8,128)(2,1)}, bf16[512,128]{1,0:T(8,128)(2,1)S(1)}, u32[]{:S(2)}) copy-start(bf16[512,128]{1,0:T(8,128)(2,1)S(1)} %collective-permute-done.1) | copy-start | bytes 393220
  53.4 2.4 %copy-start.9 = (bf16[512,128]{1,0:T(8,128)(2,1)}, bf16[512,128]{1,0:T(8,128)(2,1)S(1)}, u32[]{:S(2)}) copy-start(bf16[512,128]{1,0:T(8,128)(2,1)S(1)} %collective-permute-done) | copy-start | bytes 393220
  58.5 11.7 %copy-start.4 = (bf16[64,8,128]{2,0,1:T(8,128)(2,1)S(1)}, bf16[64,8,128]{2,0,1:T(8,128)(2,1)}, u32[]{:S(2)}) copy-start(bf16[64,8,128]{2,0,1:T(8,128)(2,1)} %copy-done.3) | copy-start | bytes 393220
  60.0 36.2 %collective-permute-start.6 = (f32[512,128]{0,1:T(8,128)}, f32[512,128]{0,1:T(8,128)S(1)}, u32[]{:S(2)}, u32[]{:S(2)}) collective-permute-start(f32[512,128]{0,1:T(8,128)} %fusion.63), channel_id=1, source_target_pairs={{8,0},{16,8},{24,16},{32,24},{40,32},{48,40},{56,48},{64,56},{72,6... | collective-permute-start | bytes 786440 | tf_op jit(solution)/shard_map/ppermute | solution.py:17
  62.1 10.0 %copy-start.2 = (f32[512,512]{0,1:T(8,128)S(1)}, f32[512,512]{0,1:T(8,128)}, u32[]{:S(2)}) copy-start(f32[512,512]{0,1:T(8,128)} %copy.132) | copy-start | bytes 3145732
  63.6 33.2 %collective-permute-start.7 = (f32[512,128]{0,1:T(8,128)}, f32[512,128]{0,1:T(8,128)}, u32[]{:S(2)}, u32[]{:S(2)}) collective-permute-start(f32[512,128]{0,1:T(8,128)} %fusion.66), channel_id=1, source_target_pairs={{16,0},{24,8},{32,16},{40,24},{48,32},{56,40},{64,48},{72,56},{80,... | collective-permute-start | bytes 786440 | tf_op jit(solution)/shard_map/ppermute | solution.py:17
  75.1 14.5 %copy-start.1 = (bf16[1,4,512,512]{2,3,1,0:T(8,128)(2,1)}, bf16[1,4,512,512]{2,3,1,0:T(8,128)(2,1)S(1)}, u32[]{:S(2)}) copy-start(bf16[1,4,512,512]{2,3,1,0:T(8,128)(2,1)S(1)} %fusion.5) | copy-start | bytes 6291460
  78.6 11.1 %copy-start.6 = (bf16[64,8,128]{2,0,1:T(8,128)(2,1)S(1)}, bf16[64,8,128]{2,0,1:T(8,128)(2,1)}, u32[]{:S(2)}) copy-start(bf16[64,8,128]{2,0,1:T(8,128)(2,1)} %copy-done.5) | copy-start | bytes 393220
  78.6 20.9 %collective-permute-start.4 = (f32[512,128]{1,0:T(8,128)}, f32[512,128]{1,0:T(8,128)}, u32[]{:S(2)}, u32[]{:S(2)}) collective-permute-start(f32[512,128]{1,0:T(8,128)} %fusion.81), channel_id=1, source_target_pairs={{8,0},{16,8},{24,16},{32,24},{40,32},{48,40},{56,48},{64,56},{72,6... | collective-permute-start | bytes 786440 | tf_op jit(solution)/shard_map/ppermute | solution.py:17
  84.5 5.6 %copy-start.8 = (bf16[512,128]{1,0:T(8,128)(2,1)S(1)}, bf16[512,128]{1,0:T(8,128)(2,1)}, u32[]{:S(2)}) copy-start(bf16[512,128]{1,0:T(8,128)(2,1)} %copy-done.7) | copy-start | bytes 393220
  84.5 6.1 %copy-start.10 = (bf16[512,128]{1,0:T(8,128)(2,1)S(1)}, bf16[512,128]{1,0:T(8,128)(2,1)}, u32[]{:S(2)}) copy-start(bf16[512,128]{1,0:T(8,128)(2,1)} %copy-done.9) | copy-start | bytes 393220
  86.0 13.5 %collective-permute-start.5 = (f32[512,128]{1,0:T(8,128)}, f32[512,128]{1,0:T(8,128)}, u32[]{:S(2)}, u32[]{:S(2)}) collective-permute-start(f32[512,128]{1,0:T(8,128)} %fusion.78), channel_id=1, source_target_pairs={{16,0},{24,8},{32,16},{40,24},{48,32},{56,40},{64,48},{72,56},{80,... | collective-permute-start | bytes 786440 | tf_op jit(solution)/shard_map/ppermute | solution.py:17
  96.2 0.7 copy-start.11
where the time goes:
time: 104 us; the launch traced here: 103 us
  starting transfers between devices  47.3 us (45%)
  matrix products  24.2 us (23%)
  local copies, waits for them, and re-layouts  12.9 us (12%)
  other arithmetic  10.3 us (10%)
  between operations  4.03 us (4%)
  waiting for transfers between devices  3.71 us (4%)
    ppermute x8, starting transfers between devices, from_behind(): return lax.ppermute(array, axis, pairs)  32.3 us
    unnamed x27, local copies, waits for them, and re-layouts  6.49 us
    dot_general x3, matrix products, tile_grads(): jnp.einsum('kgts,tkgd->skd', dscore, query_heads, preferred_element_type=...  5.89 us
    all_to_all x1, starting transfers between devices, per_device(): lax.all_to_all(keys, 'head', split_axis=1, concat_axis=0, tiled=True)  5.37 us
    all_to_all x1, starting transfers between devices, per_device(): lax.all_to_all(values, 'head', split_axis=1, concat_axis=0, tiled=True)  5.16 us
    dot_general x3, matrix products, tile_grads(): jnp.einsum('kgts,tkgd->skd', probs, grad_heads, preferred_element_type=jn...  4.83 us
    dot_general x3, matrix products, tile_grads(): jnp.einsum('tkgd,skd->kgts', grad_heads, value_heads(value_block), prefer...  4.69 us
    all_to_all x1, starting transfers between devices, per_device(): lax.all_to_all(queries, 'head', split_axis=1, concat_axis=0, tiled=True)  4.48 us
  transfers between devices with their start and end apart: 11, of which 1 were waited for; matrix products, arithmetic and copies ran while one was open for 41% of the time, Pallas kernels for 0%

commit v1 on v0

v1 whole, which is shorter than its diff:
```python
import math

import jax
import jax.numpy as jnp
from jax import lax
from jax.experimental import pallas as pl
from jax.experimental.pallas import tpu as pltpu
from jax.sharding import PartitionSpec as P

F32 = jnp.float32
BF16 = jnp.bfloat16
TOKENS = 512
HEADS = 4
SIZE = 128
PIECE = 64
PEERS = 8
BLOCK = 256
CHUNKS = 4
CHUNK = TOKENS // CHUNKS
SCALE = 1.0 / math.sqrt(SIZE)
EXP_SCALE = math.log2(math.e) * SCALE
NEGATIVE = -1e30
MESH = pl.DeviceIdType.MESH
STEPS = [(1, 0), (1, 1), (1, 3), (1, 2), (0, 1), (0, 3), (0, 2)]


def dot(a, b, transposed=False):
    dims = (((1,), (1 if transposed else 0,)), ((), ()))
    return lax.dot_general(a, b, dims, preferred_element_type=F32)


def ancestor_seen(parents_ref, segment):
    first = parents_ref[segment]
    second = jnp.where(first >= 0, parents_ref[jnp.maximum(first, 0)], -1)
    seen = []
    for gap in (1, 2):
        wanted = segment - gap
        seen.append((wanted >= 0) & ((first == wanted) | (second == wanted)))
    return seen


def kernel(
    q_hbm, k_hbm, v_hbm, up_hbm, mask_ref, parents_ref, count_ref,
    att_hbm, dq_hbm, dk_hbm, dv_hbm,
    q_in, kv, up, stacked_q, stacked_g, kv_t, probs, scores, delta, dq_t, dscore,
    att, dq, ret_tx, ret_rx, own_grad, own_out,
    kv_sem, q_sem, gap_sem, ret_sem, send_sem, local_sem,
):
    segment = lax.axis_index("seq")
    group = lax.axis_index("head")
    odd = segment % 2
    sibling = segment + 1 - 2 * odd
    last = 64
    x, y = group // 4, group % 4

    my_rows = pl.ds(pl.multiple_of(group * PIECE, PIECE), PIECE)
    my_kv_cols = pl.ds(pl.multiple_of(group * SIZE, SIZE), SIZE)
    my_q_cols = pl.ds(pl.multiple_of(group * HEADS * SIZE, HEADS * SIZE), HEADS * SIZE)
    my_chunk = group // (CHUNK // PIECE)
    own_copies = [
        pltpu.make_async_copy(k_hbm.at[:, my_kv_cols], kv.at[0, 0, my_rows, :], local_sem.at[0]),
        pltpu.make_async_copy(v_hbm.at[:, my_kv_cols], kv.at[0, 1, my_rows, :], local_sem.at[1]),
        pltpu.make_async_copy(q_hbm.at[:, my_q_cols], q_in.at[my_rows, :], local_sem.at[2]),
        pltpu.make_async_copy(up_hbm, up, local_sem.at[3]),
    ]
    for copy in own_copies:
        copy.start()

    barrier = pltpu.get_barrier_semaphore()
    peers = []
    for x_step, y_step in STEPS:
        peer = (x + x_step) % 2 * 4 + (y + y_step) % 4
        peers.append(peer)
        pl.semaphore_signal(barrier, inc=1, device_id={"head": peer}, device_id_type=MESH)
    pl.semaphore_signal(barrier, inc=1, device_id={"seq": sibling}, device_id_type=MESH)
    has_next = segment < last - 2
    has_before = segment >= 2

    for other in ((segment + 2) % last, (segment + last - 2) % last):
        pl.semaphore_signal(barrier, inc=1, device_id={"seq": other}, device_id_type=MESH)
    pl.semaphore_wait(barrier, 10)

    sends = []

    def send(src, dst, recv, device):
        copy = pltpu.make_async_remote_copy(
            src_ref=src, dst_ref=dst, send_sem=send_sem.at[len(sends)], recv_sem=recv,
            device_id=device, device_id_type=MESH,
        )
        copy.start()
        sends.append(copy)

    for n, peer in enumerate(peers):
        cols = pl.ds(pl.multiple_of(peer * SIZE, SIZE), SIZE)
        send(k_hbm.at[:, cols], kv.at[0, 0, my_rows, :], kv_sem.at[0, group], {"head": peer})
        send(v_hbm.at[:, cols], kv.at[0, 1, my_rows, :], kv_sem.at[1, group], {"head": peer})
    for n, peer in enumerate(peers):
        cols = pl.ds(pl.multiple_of(peer * HEADS * SIZE, HEADS * SIZE), HEADS * SIZE)
        send(q_hbm.at[:, cols], q_in.at[my_rows, :], q_sem.at[group], {"head": peer})

    def wait_for(ref, sem):
        pltpu.make_async_copy(ref, ref, sem).wait()

    own_copies[0].wait()
    own_copies[1].wait()

    def to_next(c, start):
        rows = pl.ds(c * CHUNK, CHUNK)
        return pltpu.make_async_remote_copy(
            src_ref=kv.at[0, :, rows, :], dst_ref=kv.at[2, :, rows, :],
            send_sem=send_sem.at[32 + c], recv_sem=gap_sem.at[1, c],
            device_id={"seq": segment + 2}, device_id_type=MESH,
        )

    def to_sibling(c, source):
        rows = pl.ds(c * CHUNK, CHUNK)
        return pltpu.make_async_remote_copy(
            src_ref=kv.at[source, :, rows, :], dst_ref=kv.at[1, :, rows, :],
            send_sem=send_sem.at[36 + c], recv_sem=gap_sem.at[0, c],
            device_id={"seq": sibling}, device_id_type=MESH,
        )

    for c in range(CHUNKS):
        for r in range(c * CHUNK // PIECE, (c + 1) * CHUNK // PIECE):

            @pl.when(group != r)
            def _():
                wait_for(kv.at[0, 0, pl.ds(r * PIECE, PIECE), :], kv_sem.at[0, r])
                wait_for(kv.at[0, 1, pl.ds(r * PIECE, PIECE), :], kv_sem.at[1, r])

        @pl.when(has_next)
        def _():
            to_next(c, True).start()

        @pl.when(odd == 0)
        def _():
            to_sibling(c, 0).start()

    for c in range(CHUNKS):

        @pl.when(has_before)
        def _():
            wait_for(kv.at[2, :, pl.ds(c * CHUNK, CHUNK), :], gap_sem.at[1, c])

        @pl.when(has_before & (odd == 1))
        def _():
            to_sibling(c, 2).start()

    @pl.when(segment < 2)
    def _():
        kv[2] = jnp.zeros(kv.shape[1:], BF16)

    @pl.when(segment == 0)
    def _():
        kv[1] = jnp.zeros(kv.shape[1:], BF16)

    own_copies[2].wait()
    for r in range(PEERS):

        @pl.when(group != r)
        def _():
            wait_for(q_in.at[pl.ds(r * PIECE, PIECE), :], q_sem.at[r])

    for h in range(HEADS):
        stacked_q[h * TOKENS : (h + 1) * TOKENS, :] = q_in[:, h * SIZE : (h + 1) * SIZE]

    @pl.when(segment > 0)
    def _():
        for c in range(CHUNKS):
            wait_for(kv.at[1, :, pl.ds(c * CHUNK, CHUNK), :], gap_sem.at[0, c])

    for t in range(3):
        for i in range(2):
            kv_t[t, i] = kv[t, i].T
    own_copies[3].wait()

    seen = ancestor_seen(parents_ref, segment)
    weight = mask_ref[...].astype(F32) / count_ref[0].astype(F32)
    causal = lax.broadcasted_iota(jnp.int32, (BLOCK, BLOCK), 0) <= lax.broadcasted_iota(
        jnp.int32, (BLOCK, BLOCK), 1
    )
    for half in range(2):
        tok = slice(half * BLOCK, (half + 1) * BLOCK)
        tiles = [(2, 0), (2, BLOCK), (1, 0), (1, BLOCK)] + [(0, r) for r in range(0, (half + 1) * BLOCK, BLOCK)]
        for h in range(HEADS):
            rows = slice(h * TOKENS + half * BLOCK, h * TOKENS + (half + 1) * BLOCK)
            cols = slice(h * SIZE, (h + 1) * SIZE)
            slot = h % 2
            query = stacked_q[rows, :]
            tops = [None, None, None]
            for n, (t, r) in enumerate(tiles):
                s = dot(kv[t, 0, r : r + BLOCK, :], query, transposed=True)
                if t == 0 and r == half * BLOCK:
                    s = jnp.where(causal, s, NEGATIVE)
                scores[slot, n] = s
                top = jnp.max(s.reshape(BLOCK // 8, 8, BLOCK), axis=0)
                tops[t] = top if tops[t] is None else jnp.maximum(tops[t], top)
            top = tops[0]
            for gap in (1, 2):
                top = jnp.maximum(top, jnp.where(seen[gap - 1], tops[gap], NEGATIVE))
            top = jnp.max(top, axis=0, keepdims=True) * EXP_SCALE
            shifts = [top] + [jnp.where(seen[gap - 1], top, -NEGATIVE) for gap in (1, 2)]
            total, out = None, None
            for n, (t, r) in enumerate(tiles):
                e = jnp.exp2(scores[slot, n] * EXP_SCALE - shifts[t])
                part = jnp.sum(e.reshape(BLOCK // 8, 8, BLOCK), axis=0)
                total = part if total is None else total + part
                e = e.astype(BF16)
                probs[t, r : r + BLOCK, rows] = e
                o = dot(kv_t[t, 1, :, r : r + BLOCK], e)
                out = o if out is None else out + o
            inverse = 1.0 / jnp.sum(total, axis=0, keepdims=True)
            out = (out * inverse).T.astype(BF16)
            att[tok, cols] = out
            factor = jnp.broadcast_to(weight[0:1, tok] * inverse, (SIZE, BLOCK)).T
            g = (up[tok, cols].astype(F32) * factor).astype(BF16)
            stacked_g[rows, :] = g
            product = (g.astype(F32) * out.astype(F32)).T
            delta[0:1, rows] = jnp.sum(product, axis=0, keepdims=True)
    att_out = pltpu.make_async_copy(att, att_hbm, local_sem.at[4])
    att_out.start()

    def backward(t, first):
        def step(n):
            rows = slice(n * BLOCK, (n + 1) * BLOCK)
            d = dot(kv[t, 1], stacked_g[rows, :], transposed=True)
            d = (probs[t, :, rows].astype(F32) * (d - delta[0:1, rows])).astype(BF16)
            dscore[:, rows] = d
            part = dot(kv_t[t, 0], d)
            dq_t[:, rows] = part if first else dq_t[:, rows] + part

        for n in range(2 * HEADS):
            step(n)
        return dot(dscore[...], stacked_q[...]) * SCALE, dot(probs[t], stacked_g[...])

    dk, dv = backward(1 + odd, True)
    ret_tx[0, 0] = dk.astype(BF16)
    ret_tx[0, 1] = dv.astype(BF16)

    def part_copy(slot):
        return pltpu.make_async_remote_copy(
            src_ref=ret_tx.at[slot], dst_ref=ret_rx.at[0],
            send_sem=send_sem.at[40 + slot], recv_sem=ret_sem.at[0],
            device_id={"seq": sibling}, device_id_type=MESH,
        )

    def back_copy(slot):
        return pltpu.make_async_remote_copy(
            src_ref=ret_tx.at[slot], dst_ref=ret_rx.at[1],
            send_sem=send_sem.at[42 + slot], recv_sem=ret_sem.at[1],
            device_id={"seq": segment - 2}, device_id_type=MESH,
        )

    @pl.when(odd == 0)
    def _():
        part_copy(0).start()

    @pl.when(odd == 1)
    def _():
        wait_for(ret_rx.at[0], ret_sem.at[0])
        for i in range(2):
            ret_tx[0, i] = (ret_tx[0, i].astype(F32) + ret_rx[0, i].astype(F32)).astype(BF16)

    @pl.when((odd == 1) & has_before)
    def _():
        back_copy(0).start()

    dk, dv = backward(2 - odd, False)
    ret_tx[1, 0] = dk.astype(BF16)
    ret_tx[1, 1] = dv.astype(BF16)

    @pl.when(odd == 1)
    def _():
        part_copy(1).start()

    @pl.when((odd == 0) & has_before)
    def _():
        back_copy(1).start()

    for half in range(2):
        seen_rows = (half + 1) * BLOCK
        tok = slice(half * BLOCK, (half + 1) * BLOCK)
        for h in range(HEADS):
            rows = slice(h * TOKENS + half * BLOCK, h * TOKENS + (half + 1) * BLOCK)
            d = dot(kv[0, 1, 0:seen_rows, :], stacked_g[rows, :], transposed=True)
            d = (probs[0, 0:seen_rows, rows].astype(F32) * (d - delta[0:1, rows])).astype(BF16)
            dscore[0:seen_rows, rows] = d
            total = dq_t[:, rows] + dot(kv_t[0, 0, :, 0:seen_rows], d)
            dq[tok, h * SIZE : (h + 1) * SIZE] = (total * SCALE).T.astype(BF16)
    dq_out = pltpu.make_async_copy(dq, dq_hbm, local_sem.at[5])
    dq_out.start()
    own_grad[0, 0:BLOCK] = dot(dscore[0:BLOCK, :], stacked_q[...]) * SCALE
    own_grad[1, 0:BLOCK] = dot(probs[0, 0:BLOCK, :], stacked_g[...])
    dk, dv = None, None
    for h in range(HEADS):
        rows = slice(h * TOKENS + BLOCK, (h + 1) * TOKENS)
        a = dot(dscore[BLOCK:, rows], stacked_q[rows, :])
        b = dot(probs[0, BLOCK:, rows], stacked_g[rows, :])
        dk = a if dk is None else dk + a
        dv = b if dv is None else dv + b
    own_grad[0, BLOCK:] = dk * SCALE
    own_grad[1, BLOCK:] = dv

    @pl.when(odd == 0)
    def _():
        wait_for(ret_rx.at[0], ret_sem.at[0])
        for i in range(2):
            own_grad[i] = own_grad[i] + ret_rx[0, i].astype(F32)

    @pl.when(has_next)
    def _():
        wait_for(ret_rx.at[1], ret_sem.at[1])
        for i in range(2):
            own_grad[i] = own_grad[i] + ret_rx[1, i].astype(F32)

    for i in range(2):
        own_out[i] = own_grad[i].astype(BF16)
    outs = [
        pltpu.make_async_copy(own_out.at[0], dk_hbm, local_sem.at[6]),
        pltpu.make_async_copy(own_out.at[1], dv_hbm, local_sem.at[7]),
    ]
    for copy in outs:
        copy.start()

    for copy in sends:
        copy.wait_send()
    for c in range(CHUNKS):

        @pl.when(has_next)
        def _():
            to_next(c, False).wait_send()

        @pl.when((odd == 0) | has_before)
        def _():
            to_sibling(c, 0).wait_send()

    @pl.when(odd == 0)
    def _():
        part_copy(0).wait_send()

    @pl.when(odd == 1)
    def _():
        part_copy(1).wait_send()

    @pl.when((odd == 1) & has_before)
    def _():
        back_copy(0).wait_send()

    @pl.when((odd == 0) & has_before)
    def _():
        back_copy(1).wait_send()

    att_out.wait()
    dq_out.wait()
    for copy in outs:
        copy.wait()


def per_device(queries, keys, values, upstream, loss_mask, parents, token_count):
    hbm = pl.BlockSpec(memory_space=pl.ANY)
    smem = pl.BlockSpec(memory_space=pltpu.SMEM)
    wide = jax.ShapeDtypeStruct((TOKENS, HEADS * SIZE), BF16)
    narrow = jax.ShapeDtypeStruct((TOKENS, SIZE), BF16)
    rows = HEADS * TOKENS
    return pl.pallas_call(
        kernel,
        out_shape=(wide, wide, narrow, narrow),
        in_specs=[hbm, hbm, hbm, hbm, pl.BlockSpec(memory_space=pltpu.VMEM), smem, smem],
        out_specs=[hbm] * 4,
        scratch_shapes=[
            pltpu.VMEM((TOKENS, HEADS * SIZE), BF16),
            pltpu.VMEM((3, 2, TOKENS, SIZE), BF16),
            pltpu.VMEM((TOKENS, HEADS * SIZE), BF16),
            pltpu.VMEM((rows, SIZE), BF16),
            pltpu.VMEM((rows, SIZE), BF16),
            pltpu.VMEM((3, 2, SIZE, TOKENS), BF16),
            pltpu.VMEM((3, TOKENS, rows), BF16),
            pltpu.VMEM((2, 6, BLOCK, BLOCK), F32),
            pltpu.VMEM((8, rows), F32),
            pltpu.VMEM((SIZE, rows), F32),
            pltpu.VMEM((TOKENS, rows), BF16),
            pltpu.VMEM((TOKENS, HEADS * SIZE), BF16),
            pltpu.VMEM((TOKENS, HEADS * SIZE), BF16),
            pltpu.VMEM((2, 2, TOKENS, SIZE), BF16),
            pltpu.VMEM((2, 2, TOKENS, SIZE), BF16),
            pltpu.VMEM((2, TOKENS, SIZE), F32),
            pltpu.VMEM((2, TOKENS, SIZE), BF16),
            pltpu.SemaphoreType.DMA((2, PEERS)),
            pltpu.SemaphoreType.DMA((PEERS,)),
            pltpu.SemaphoreType.DMA((2, CHUNKS)),
            pltpu.SemaphoreType.DMA((2,)),
            pltpu.SemaphoreType.DMA((44,)),
            pltpu.SemaphoreType.DMA((8,)),
        ],
        compiler_params=pltpu.CompilerParams(
            collective_id=0, has_side_effects=True, vmem_limit_bytes=62 << 20
        ),
        cost_estimate=pl.CostEstimate(flops=5 * 10**9, bytes_accessed=3 * 10**6, transcendentals=3 * 10**6),
    )(queries, keys, values, upstream, loss_mask.reshape(1, TOKENS), parents, token_count)


def solution(mesh):
    in_specs = (
        P(("seq", "head"), None),
        P(("seq", "head"), None),
        P(("seq", "head"), None),
        P("seq", "head"),
        P("seq"),
        P(),
        P(),
    )
    out_specs = (P("seq", "head"), P("seq", "head"), P("seq", "head"), P("seq", "head"))
    return jax.shard_map(
        per_device, mesh=mesh, in_specs=in_specs, out_specs=out_specs, check_vma=False
    )
```

time: 104 us -> 58.3 us (0.56)
  the two profiles are of different devices: /device:TPU:7 before, /device:TPU:2 now
where the time goes in v1:
time: 58.3 us; the launch traced here: 58.1 us
  Pallas kernels  52.2 us (90%)
  local copies, waits for them, and re-layouts  4.56 us (8%)
  between operations  1.3 us (2%)
    pallas_call x1, Pallas kernels, per_device(): pl.pallas_call(kernel, out_shape=(wide, wide, narrow, narrow), in_specs=[...  52.2 us
    unnamed x10, local copies, waits for them, and re-layouts  4.56 us

profile of v1, /device:TPU:2, one launch (start us, length us, event | category | flops | bytes accessed | tf_op | source)
XLA Modules:
  0.0 58.1 jit_solution(7717438595030858661)
XLA Ops:
  1.3 52.2 %shard_map.102 = (bf16[512,512]{1,0:T(8,128)(2,1)}, bf16[512,512]{1,0:T(8,128)(2,1)}, bf16[512,128]{1,0:T(8,128)(2,1)}, bf16[512,128]{1,0:T(8,128)(2,1)}) custom-call(bf16[64,4096]{1,0:T(8,128)(2,1)} %q_hbm.1, bf16[64,1024]{1,0:T(8,128)(2,1)} %k_hbm.1, bf16[64,1024]{1,0:T(8,128)(2,1)} %v_hbm.1, bf16[512,512]{1,0:T(8,128)(2,1)} %up_hbm.1, s32[1,512]{1,0:T(1,128)} %bitcast.1, ...), custom_call_target="tpu_custom_call" | custom-call | flops 5000000000 | bytes 3000000 | tf_op jit(solution)/shard_map/pallas_call | solution.py:365
  53.5 0.0 copy-start
  53.5 1.9 %copy.16 = bf16[512,512]{1,0:T(8,128)(2,1)} copy(bf16[512,512]{1,0:T(8,128)(2,1)} %get-tuple-element.8) | data formatting | bytes 1048576
  55.4 0.0 copy-done
  55.4 0.0 copy-start.2
  55.4 0.8 %copy.17 = bf16[512,512]{1,0:T(8,128)(2,1)} copy(bf16[512,512]{1,0:T(8,128)(2,1)S(1)} %copy-done) | data formatting | bytes 1048576
  56.2 0.2 copy-done.2
  56.5 0.0 copy-start.1
  56.5 0.7 %copy.18 = bf16[512,128]{1,0:T(8,128)(2,1)} copy(bf16[512,128]{1,0:T(8,128)(2,1)S(1)} %copy-done.2) | data formatting | bytes 262144
  57.1 0.3 copy-done.1
  57.4 0.7 %copy.19 = bf16[512,128]{1,0:T(8,128)(2,1)} copy(bf16[512,128]{1,0:T(8,128)(2,1)S(1)} %copy-done.1) | data formatting | bytes 262144
Async XLA Ops:
  53.5 1.9 %copy-start = (bf16[512,512]{1,0:T(8,128)(2,1)S(1)}, bf16[512,512]{1,0:T(8,128)(2,1)}, u32[]{:S(2)}) copy-start(bf16[512,512]{1,0:T(8,128)(2,1)} %get-tuple-element.9) | copy-start | bytes 1572868
  55.4 1.0 %copy-start.2 = (bf16[512,128]{1,0:T(8,128)(2,1)S(1)}, bf16[512,128]{1,0:T(8,128)(2,1)}, u32[]{:S(2)}) copy-start(bf16[512,128]{1,0:T(8,128)(2,1)} %get-tuple-element.10) | copy-start | bytes 393220
  56.5 1.0 %copy-start.1 = (bf16[512,128]{1,0:T(8,128)(2,1)S(1)}, bf16[512,128]{1,0:T(8,128)(2,1)}, u32[]{:S(2)}) copy-start(bf16[512,128]{1,0:T(8,128)(2,1)} %get-tuple-element.11) | copy-start | bytes 393220

commit v2 on v1

--- a/solution.py
+++ b/solution.py
@@ -40,11 +40,11 @@
 
 
 def kernel(
-    q_hbm, k_hbm, v_hbm, up_hbm, mask_ref, parents_ref, count_ref,
-    att_hbm, dq_hbm, dk_hbm, dv_hbm,
+    q_hbm, k_hbm, v_hbm, up_hbm, mask_hbm, parents_hbm, count_ref,
+    att, dq, dk_out, dv_out,
     q_in, kv, up, stacked_q, stacked_g, kv_t, probs, scores, delta, dq_t, dscore,
-    att, dq, ret_tx, ret_rx, own_grad, own_out,
-    kv_sem, q_sem, gap_sem, ret_sem, send_sem, local_sem,
+    ret_tx, ret_rx, own_grad, mask_ref, parents_ref,
+    kv_sem, q_sem, gap_sem, ret_sem, send_sem, edge_sem, local_sem,
 ):
     segment = lax.axis_index("seq")
     group = lax.axis_index("head")
@@ -57,11 +57,16 @@
     my_kv_cols = pl.ds(pl.multiple_of(group * SIZE, SIZE), SIZE)
     my_q_cols = pl.ds(pl.multiple_of(group * HEADS * SIZE, HEADS * SIZE), HEADS * SIZE)
     my_chunk = group // (CHUNK // PIECE)
+    chip = segment // 2
+    edge_source = chip // 15 - chip // 16 - chip // 30
+    edge_target = chip // 16 - chip // 17
     own_copies = [
         pltpu.make_async_copy(k_hbm.at[:, my_kv_cols], kv.at[0, 0, my_rows, :], local_sem.at[0]),
         pltpu.make_async_copy(v_hbm.at[:, my_kv_cols], kv.at[0, 1, my_rows, :], local_sem.at[1]),
         pltpu.make_async_copy(q_hbm.at[:, my_q_cols], q_in.at[my_rows, :], local_sem.at[2]),
         pltpu.make_async_copy(up_hbm, up, local_sem.at[3]),
+        pltpu.make_async_copy(mask_hbm, mask_ref, local_sem.at[4]),
+        pltpu.make_async_copy(parents_hbm, parents_ref, local_sem.at[5]),
     ]
     for copy in own_copies:
         copy.start()
@@ -76,11 +81,46 @@
     has_next = segment < last - 2
     has_before = segment >= 2
 
-    for other in ((segment + 2) % last, (segment + last - 2) % last):
-        pl.semaphore_signal(barrier, inc=1, device_id={"seq": other}, device_id_type=MESH)
-    pl.semaphore_wait(barrier, 10)
+
+    def signal(**device):
+        pl.semaphore_signal(barrier, inc=1, device_id=device, device_id_type=MESH)
+
+    @pl.when(has_next & (edge_source == 0))
+    def _():
+        signal(seq=segment + 2)
+
+    @pl.when(has_before & (edge_target == 0))
+    def _():
+        signal(seq=segment - 2)
+
+    @pl.when(edge_source == 1)
+    def _():
+        for peer in range(PEERS):
+            signal(seq=segment + 2, head=peer)
+
+    @pl.when(edge_target == 1)
+    def _():
+        for peer in range(PEERS):
+            signal(seq=segment - 2, head=peer)
+
+    near = (segment + last - 2) // last + (2 * last - 3 - segment) // last
+    pl.semaphore_wait(barrier, 8 + near + 7 * (edge_source + edge_target))
 
     sends = []
+
+    def edge_copy(peer, i):
+        cols = pl.ds(peer * SIZE, SIZE)
+        return pltpu.make_async_remote_copy(
+            src_ref=(k_hbm, v_hbm)[i].at[:, cols], dst_ref=kv.at[2, i, my_rows, :],
+            send_sem=edge_sem.at[peer, i], recv_sem=gap_sem.at[1, my_chunk],
+            device_id={"seq": segment + 2, "head": peer}, device_id_type=MESH,
+        )
+
+    @pl.when(edge_source == 1)
+    def _():
+        for peer in range(PEERS):
+            for i in range(2):
+                edge_copy(peer, i).start()
 
     def send(src, dst, recv, device):
         copy = pltpu.make_async_remote_copy(
@@ -104,43 +144,48 @@
     own_copies[0].wait()
     own_copies[1].wait()
 
-    def to_next(c, start):
-        rows = pl.ds(c * CHUNK, CHUNK)
+    order = [(n + x * (CHUNKS // 2)) % CHUNKS for n in range(CHUNKS)]
+
+    def chunk_rows(c):
+        return pl.ds(pl.multiple_of(c * CHUNK, CHUNK), CHUNK)
+
+    def to_next(c):
         return pltpu.make_async_remote_copy(
-            src_ref=kv.at[0, :, rows, :], dst_ref=kv.at[2, :, rows, :],
+            src_ref=kv.at[0, :, chunk_rows(c), :], dst_ref=kv.at[2, :, chunk_rows(c), :],
             send_sem=send_sem.at[32 + c], recv_sem=gap_sem.at[1, c],
             device_id={"seq": segment + 2}, device_id_type=MESH,
         )
 
     def to_sibling(c, source):
-        rows = pl.ds(c * CHUNK, CHUNK)
         return pltpu.make_async_remote_copy(
-            src_ref=kv.at[source, :, rows, :], dst_ref=kv.at[1, :, rows, :],
+            src_ref=kv.at[source, :, chunk_rows(c), :], dst_ref=kv.at[1, :, chunk_rows(c), :],
             send_sem=send_sem.at[36 + c], recv_sem=gap_sem.at[0, c],
             device_id={"seq": sibling}, device_id_type=MESH,
         )
 
-    for c in range(CHUNKS):
-        for r in range(c * CHUNK // PIECE, (c + 1) * CHUNK // PIECE):
+    for c in order:
+        for n in range(CHUNK // PIECE):
+            r = c * (CHUNK // PIECE) + n
+            rows = pl.ds(pl.multiple_of(r * PIECE, PIECE), PIECE)
 
             @pl.when(group != r)
             def _():
-                wait_for(kv.at[0, 0, pl.ds(r * PIECE, PIECE), :], kv_sem.at[0, r])
-                wait_for(kv.at[0, 1, pl.ds(r * PIECE, PIECE), :], kv_sem.at[1, r])
-
-        @pl.when(has_next)
-        def _():
-            to_next(c, True).start()
+                wait_for(kv.at[0, 0, rows, :], kv_sem.at[0, r])
+                wait_for(kv.at[0, 1, rows, :], kv_sem.at[1, r])
+
+        @pl.when(has_next & (edge_source == 0))
+        def _():
+            to_next(c).start()
 
         @pl.when(odd == 0)
         def _():
             to_sibling(c, 0).start()
 
-    for c in range(CHUNKS):
+    for c in order:
 
         @pl.when(has_before)
         def _():
-            wait_for(kv.at[2, :, pl.ds(c * CHUNK, CHUNK), :], gap_sem.at[1, c])
+            wait_for(kv.at[2, :, chunk_rows(c), :], gap_sem.at[1, c])
 
         @pl.when(has_before & (odd == 1))
         def _():
@@ -172,7 +217,8 @@
     for t in range(3):
         for i in range(2):
             kv_t[t, i] = kv[t, i].T
-    own_copies[3].wait()
+    for copy in own_copies[3:]:
+        copy.wait()
 
     seen = ancestor_seen(parents_ref, segment)
     weight = mask_ref[...].astype(F32) / count_ref[0].astype(F32)
@@ -217,65 +263,55 @@
             stacked_g[rows, :] = g
             product = (g.astype(F32) * out.astype(F32)).T
             delta[0:1, rows] = jnp.sum(product, axis=0, keepdims=True)
-    att_out = pltpu.make_async_copy(att, att_hbm, local_sem.at[4])
-    att_out.start()
-
-    def backward(t, first):
-        def step(n):
+
+    def backward(t, half, first):
+        keys = slice(half * BLOCK, (half + 1) * BLOCK)
+        for n in range(2 * HEADS):
             rows = slice(n * BLOCK, (n + 1) * BLOCK)
-            d = dot(kv[t, 1], stacked_g[rows, :], transposed=True)
-            d = (probs[t, :, rows].astype(F32) * (d - delta[0:1, rows])).astype(BF16)
-            dscore[:, rows] = d
-            part = dot(kv_t[t, 0], d)
+            d = dot(kv[t, 1, keys, :], stacked_g[rows, :], transposed=True)
+            d = (probs[t, keys, rows].astype(F32) * (d - delta[0:1, rows])).astype(BF16)
+            dscore[keys, rows] = d
+            part = dot(kv_t[t, 0, :, keys], d)
             dq_t[:, rows] = part if first else dq_t[:, rows] + part
-
-        for n in range(2 * HEADS):
-            step(n)
-        return dot(dscore[...], stacked_q[...]) * SCALE, dot(probs[t], stacked_g[...])
-
-    dk, dv = backward(1 + odd, True)
-    ret_tx[0, 0] = dk.astype(BF16)
-    ret_tx[0, 1] = dv.astype(BF16)
-
-    def part_copy(slot):
+        ret_tx[t - 1, half, 0] = (dot(dscore[keys, :], stacked_q[...]) * SCALE).astype(BF16)
+        ret_tx[t - 1, half, 1] = dot(probs[t, keys, :], stacked_g[...]).astype(BF16)
+
+    def part_copy(half):
         return pltpu.make_async_remote_copy(
-            src_ref=ret_tx.at[slot], dst_ref=ret_rx.at[0],
-            send_sem=send_sem.at[40 + slot], recv_sem=ret_sem.at[0],
+            src_ref=ret_tx.at[0, half], dst_ref=ret_rx.at[0, half],
+            send_sem=send_sem.at[40 + half], recv_sem=ret_sem.at[0, half],
             device_id={"seq": sibling}, device_id_type=MESH,
         )
 
-    def back_copy(slot):
+    def back_copy(half):
         return pltpu.make_async_remote_copy(
-            src_ref=ret_tx.at[slot], dst_ref=ret_rx.at[1],
-            send_sem=send_sem.at[42 + slot], recv_sem=ret_sem.at[1],
+            src_ref=ret_tx.at[1, half], dst_ref=ret_rx.at[1, half],
+            send_sem=send_sem.at[42 + half], recv_sem=ret_sem.at[1, half],
             device_id={"seq": segment - 2}, device_id_type=MESH,
         )
 
-    @pl.when(odd == 0)
-    def _():
-        part_copy(0).start()
-
-    @pl.when(odd == 1)
-    def _():
-        wait_for(ret_rx.at[0], ret_sem.at[0])
-        for i in range(2):
-            ret_tx[0, i] = (ret_tx[0, i].astype(F32) + ret_rx[0, i].astype(F32)).astype(BF16)
-
-    @pl.when((odd == 1) & has_before)
-    def _():
-        back_copy(0).start()
-
-    dk, dv = backward(2 - odd, False)
-    ret_tx[1, 0] = dk.astype(BF16)
-    ret_tx[1, 1] = dv.astype(BF16)
-
-    @pl.when(odd == 1)
-    def _():
-        part_copy(1).start()
-
-    @pl.when((odd == 0) & has_before)
-    def _():
-        back_copy(1).start()
+    for half in range(2):
+        backward(2, half, half == 0)
+
+        @pl.when((odd == 0) & has_before)
+        def _():
+            back_copy(half).start()
+
+    for half in range(2):
+        backward(1, half, False)
+        part_copy(half).start()
+
+    def join(half):
+        @pl.when(odd == 1)
+        def _():
+            wait_for(ret_rx.at[0, half], ret_sem.at[0, half])
+            ret_tx[1, half] = (ret_tx[1, half].astype(F32) + ret_rx[0, half].astype(F32)).astype(BF16)
+
+        @pl.when((odd == 1) & has_before)
+        def _():
+            back_copy(half).start()
+
+    join(0)
 
     for half in range(2):
         seen_rows = (half + 1) * BLOCK
@@ -287,8 +323,8 @@
             dscore[0:seen_rows, rows] = d
             total = dq_t[:, rows] + dot(kv_t[0, 0, :, 0:seen_rows], d)
             dq[tok, h * SIZE : (h + 1) * SIZE] = (total * SCALE).T.astype(BF16)
-    dq_out = pltpu.make_async_copy(dq, dq_hbm, local_sem.at[5])
-    dq_out.start()
+        if half == 0:
+            join(1)
     own_grad[0, 0:BLOCK] = dot(dscore[0:BLOCK, :], stacked_q[...]) * SCALE
     own_grad[1, 0:BLOCK] = dot(probs[0, 0:BLOCK, :], stacked_g[...])
     dk, dv = None, None
@@ -303,70 +339,74 @@
 
     @pl.when(odd == 0)
     def _():
-        wait_for(ret_rx.at[0], ret_sem.at[0])
-        for i in range(2):
-            own_grad[i] = own_grad[i] + ret_rx[0, i].astype(F32)
+        for half in range(2):
+            wait_for(ret_rx.at[0, half], ret_sem.at[0, half])
+            for i in range(2):
+                rows = slice(half * BLOCK, (half + 1) * BLOCK)
+                own_grad[i, rows] = own_grad[i, rows] + ret_rx[0, half, i].astype(F32)
 
     @pl.when(has_next)
     def _():
-        wait_for(ret_rx.at[1], ret_sem.at[1])
-        for i in range(2):
-            own_grad[i] = own_grad[i] + ret_rx[1, i].astype(F32)
-
-    for i in range(2):
-        own_out[i] = own_grad[i].astype(BF16)
-    outs = [
-        pltpu.make_async_copy(own_out.at[0], dk_hbm, local_sem.at[6]),
-        pltpu.make_async_copy(own_out.at[1], dv_hbm, local_sem.at[7]),
-    ]
-    for copy in outs:
-        copy.start()
+        for half in range(2):
+            wait_for(ret_rx.at[1, half], ret_sem.at[1, half])
+            for i in range(2):
+                rows = slice(half * BLOCK, (half + 1) * BLOCK)
+                own_grad[i, rows] = own_grad[i, rows] + ret_rx[1, half, i].astype(F32)
+
+    dk_out[...] = own_grad[0].astype(BF16)
+    dv_out[...] = own_grad[1].astype(BF16)
 
     for copy in sends:
         copy.wait_send()
+
+    @pl.when(edge_source == 1)
+    def _():
+        for peer in range(PEERS):
+            for i in range(2):
+                edge_copy(peer, i).wait_send()
+
     for c in range(CHUNKS):
 
-        @pl.when(has_next)
-        def _():
-            to_next(c, False).wait_send()
+        @pl.when(has_next & (edge_source == 0))
+        def _():
+            to_next(c).wait_send()
 
         @pl.when((odd == 0) | has_before)
         def _():
             to_sibling(c, 0).wait_send()
 
-    @pl.when(odd == 0)
-    def _():
-        part_copy(0).wait_send()
-
-    @pl.when(odd == 1)
-    def _():
-        part_copy(1).wait_send()
-
-    @pl.when((odd == 1) & has_before)
-    def _():
-        back_copy(0).wait_send()
-
-    @pl.when((odd == 0) & has_before)
-    def _():
-        back_copy(1).wait_send()
-
-    att_out.wait()
-    dq_out.wait()
-    for copy in outs:
+    for half in range(2):
+        part_copy(half).wait_send()
+
+        @pl.when(has_before)
+        def _():
+            back_copy(half).wait_send()
+
+
+def deliver(*refs):
+    copies = [pltpu.make_async_copy(refs[n], refs[n + 4], refs[8].at[n]) for n in range(4)]
+    for copy in copies:
+        copy.start()
+    for copy in copies:
         copy.wait()
 
 
 def per_device(queries, keys, values, upstream, loss_mask, parents, token_count):
-    hbm = pl.BlockSpec(memory_space=pl.ANY)
+    any_space = pl.BlockSpec(memory_space=pl.ANY)
+    hbm = pl.BlockSpec(memory_space=pltpu.HBM)
+    vmem = pl.BlockSpec(memory_space=pltpu.VMEM)
     smem = pl.BlockSpec(memory_space=pltpu.SMEM)
-    wide = jax.ShapeDtypeStruct((TOKENS, HEADS * SIZE), BF16)
-    narrow = jax.ShapeDtypeStruct((TOKENS, SIZE), BF16)
+    shapes = [(TOKENS, HEADS * SIZE)] * 2 + [(TOKENS, SIZE)] * 2
     rows = HEADS * TOKENS
-    return pl.pallas_call(
+    operands = [
+        pltpu.with_memory_space_constraint(a, pltpu.HBM)
+        for a in (queries, keys, values, upstream, loss_mask.reshape(1, TOKENS), parents)
+    ]
+    parts = pl.pallas_call(
         kernel,
-        out_shape=(wide, wide, narrow, narrow),
-        in_specs=[hbm, hbm, hbm, hbm, pl.BlockSpec(memory_space=pltpu.VMEM), smem, smem],
-        out_specs=[hbm] * 4,
+        out_shape=[pltpu.VMEM(shape, BF16) for shape in shapes],
+        in_specs=[hbm] * 4 + [any_space] * 2 + [smem],
+        out_specs=[vmem] * 4,
         scratch_shapes=[
             pltpu.VMEM((TOKENS, HEADS * SIZE), BF16),
             pltpu.VMEM((3, 2, TOKENS, SIZE), BF16),
@@ -379,24 +419,32 @@
             pltpu.VMEM((8, rows), F32),
             pltpu.VMEM((SIZE, rows), F32),
             pltpu.VMEM((TOKENS, rows), BF16),
-            pltpu.VMEM((TOKENS, HEADS * SIZE), BF16),
-            pltpu.VMEM((TOKENS, HEADS * SIZE), BF16),
-            pltpu.VMEM((2, 2, TOKENS, SIZE), BF16),
-            pltpu.VMEM((2, 2, TOKENS, SIZE), BF16),
+            pltpu.VMEM((2, 2, 2, BLOCK, SIZE), BF16),
+            pltpu.VMEM((2, 2, 2, BLOCK, SIZE), BF16),
             pltpu.VMEM((2, TOKENS, SIZE), F32),
-            pltpu.VMEM((2, TOKENS, SIZE), BF16),
+            pltpu.VMEM((1, TOKENS), jnp.int32),
+            pltpu.SMEM((64,), jnp.int32),
             pltpu.SemaphoreType.DMA((2, PEERS)),
             pltpu.SemaphoreType.DMA((PEERS,)),
             pltpu.SemaphoreType.DMA((2, CHUNKS)),
-            pltpu.SemaphoreType.DMA((2,)),
+            pltpu.SemaphoreType.DMA((2, 2)),
             pltpu.SemaphoreType.DMA((44,)),
-            pltpu.SemaphoreType.DMA((8,)),
+            pltpu.SemaphoreType.DMA((PEERS, 2)),
+            pltpu.SemaphoreType.DMA((6,)),
         ],
         compiler_params=pltpu.CompilerParams(
-            collective_id=0, has_side_effects=True, vmem_limit_bytes=62 << 20
+            collective_id=0, has_side_effects=True, vmem_limit_bytes=32 << 20
         ),
         cost_estimate=pl.CostEstimate(flops=5 * 10**9, bytes_accessed=3 * 10**6, transcendentals=3 * 10**6),
-    )(queries, keys, values, upstream, loss_mask.reshape(1, TOKENS), parents, token_count)
+    )(*operands, token_count)
+    return pl.pallas_call(
+        deliver,
+        out_shape=[jax.ShapeDtypeStruct(shape, BF16) for shape in shapes],
+        in_specs=[vmem] * 4,
+        out_specs=[hbm] * 4,
+        scratch_shapes=[pltpu.SemaphoreType.DMA((4,))],
+        compiler_params=pltpu.CompilerParams(vmem_limit_bytes=16 << 20),
+    )(*parts)
 
 
 def solution(mesh):

time: 58.3 us -> 53.4 us (0.916)
  the two profiles are of different devices: /device:TPU:2 before, /device:TPU:31 now
where the time goes in v2:
time: 53.4 us; the launch traced here: 53.2 us
  Pallas kernels  51.8 us (97%)
  between operations  1.45 us (3%)
    pallas_call x1, Pallas kernels, per_device(): pl.pallas_call(kernel, out_shape=[pltpu.VMEM(shape, BF16) for shape in sh...  50.7 us
    pallas_call x1, Pallas kernels, per_device(): pl.pallas_call(deliver, out_shape=[jax.ShapeDtypeStruct(shape, BF16) for...  1.08 us

profile of v2, /device:TPU:31, one launch (start us, length us, event | category | flops | bytes accessed | tf_op | source)
XLA Modules:
  0.0 53.2 jit_solution(546719353489565790)
XLA Ops:
  1.3 50.7 %shard_map.102 = (bf16[512,512]{1,0:T(8,128)(2,1)S(1)}, bf16[512,512]{1,0:T(8,128)(2,1)S(1)}, bf16[512,128]{1,0:T(8,128)(2,1)S(1)}, bf16[512,128]{1,0:T(8,128)(2,1)S(1)}) custom-call(bf16[64,4096]{1,0:T(8,128)(2,1)} %q_hbm.1, bf16[64,1024]{1,0:T(8,128)(2,1)} %k_hbm.1, bf16[64,1024]{1,0:T(8,128)(2,1)} %v_hbm.1, bf16[512,512]{1,0:T(8,128)(2,1)} %up_hbm.1, ...), custom_call_target="tpu_custom_call" | custom-call | flops 5000000000 | bytes 3000000 | tf_op jit(solution)/shard_map/pallas_call | solution.py:405
  52.0 1.1 %shard_map.103 = (bf16[512,512]{1,0:T(8,128)(2,1)}, bf16[512,512]{1,0:T(8,128)(2,1)}, bf16[512,128]{1,0:T(8,128)(2,1)}, bf16[512,128]{1,0:T(8,128)(2,1)}) custom-call(bf16[512,512]{1,0:T(8,128)(2,1)S(1)} %get-tuple-element.8.refs_0_, bf16[512,512]{1,0:T(8,128)(2,1)S(1)} %get-tuple-element.9.refs_1_, bf16[512,128]{1,0:T(8,128)(2,1)S(1)} %get-tuple-element.10.refs_2_, ...), custom_call_target="tpu_custom_call" | custom-call | tf_op jit(solution)/shard_map/pallas_call | solution.py:440

commit v3 on v2

--- a/solution.py
+++ b/solution.py
@@ -24,8 +24,8 @@
 STEPS = [(1, 0), (1, 1), (1, 3), (1, 2), (0, 1), (0, 3), (0, 2)]
 
 
-def dot(a, b, transposed=False):
-    dims = (((1,), (1 if transposed else 0,)), ((), ()))
+def dot(a, b, left=1, right=0):
+    dims = (((left,), (right,)), ((), ()))
     return lax.dot_general(a, b, dims, preferred_element_type=F32)
 
 
@@ -42,7 +42,7 @@
 def kernel(
     q_hbm, k_hbm, v_hbm, up_hbm, mask_hbm, parents_hbm, count_ref,
     att, dq, dk_out, dv_out,
-    q_in, kv, up, stacked_q, stacked_g, kv_t, probs, scores, delta, dq_t, dscore,
+    q_in, kv, up, stacked_q, stacked_g, v_t, probs, scores, delta, dscore,
     ret_tx, ret_rx, own_grad, mask_ref, parents_ref,
     kv_sem, q_sem, gap_sem, ret_sem, send_sem, edge_sem, local_sem,
 ):
@@ -61,8 +61,8 @@
     edge_source = chip // 15 - chip // 16 - chip // 30
     edge_target = chip // 16 - chip // 17
     own_copies = [
-        pltpu.make_async_copy(k_hbm.at[:, my_kv_cols], kv.at[0, 0, my_rows, :], local_sem.at[0]),
-        pltpu.make_async_copy(v_hbm.at[:, my_kv_cols], kv.at[0, 1, my_rows, :], local_sem.at[1]),
+        pltpu.make_async_copy(k_hbm.at[:, my_kv_cols], kv.at[0, my_rows, :], local_sem.at[0]),
+        pltpu.make_async_copy(v_hbm.at[:, my_kv_cols], kv.at[1, my_rows, :], local_sem.at[1]),
         pltpu.make_async_copy(q_hbm.at[:, my_q_cols], q_in.at[my_rows, :], local_sem.at[2]),
         pltpu.make_async_copy(up_hbm, up, local_sem.at[3]),
         pltpu.make_async_copy(mask_hbm, mask_ref, local_sem.at[4]),
@@ -85,33 +85,23 @@
     def signal(**device):
         pl.semaphore_signal(barrier, inc=1, device_id=device, device_id_type=MESH)
 
-    @pl.when(has_next & (edge_source == 0))
-    def _():
-        signal(seq=segment + 2)
-
     @pl.when(has_before & (edge_target == 0))
     def _():
         signal(seq=segment - 2)
-
-    @pl.when(edge_source == 1)
-    def _():
-        for peer in range(PEERS):
-            signal(seq=segment + 2, head=peer)
 
     @pl.when(edge_target == 1)
     def _():
         for peer in range(PEERS):
             signal(seq=segment - 2, head=peer)
 
-    near = (segment + last - 2) // last + (2 * last - 3 - segment) // last
-    pl.semaphore_wait(barrier, 8 + near + 7 * (edge_source + edge_target))
+    pl.semaphore_wait(barrier, 8 + (2 * last - 3 - segment) // last + 7 * edge_source)
 
     sends = []
 
     def edge_copy(peer, i):
         cols = pl.ds(peer * SIZE, SIZE)
         return pltpu.make_async_remote_copy(
-            src_ref=(k_hbm, v_hbm)[i].at[:, cols], dst_ref=kv.at[2, i, my_rows, :],
+            src_ref=(k_hbm, v_hbm)[i].at[:, cols], dst_ref=kv.at[i, pl.ds(pl.multiple_of(2 * TOKENS + group * PIECE, PIECE), PIECE), :],
             send_sem=edge_sem.at[peer, i], recv_sem=gap_sem.at[1, my_chunk],
             device_id={"seq": segment + 2, "head": peer}, device_id_type=MESH,
         )
@@ -132,8 +122,8 @@
 
     for n, peer in enumerate(peers):
         cols = pl.ds(pl.multiple_of(peer * SIZE, SIZE), SIZE)
-        send(k_hbm.at[:, cols], kv.at[0, 0, my_rows, :], kv_sem.at[0, group], {"head": peer})
-        send(v_hbm.at[:, cols], kv.at[0, 1, my_rows, :], kv_sem.at[1, group], {"head": peer})
+        send(k_hbm.at[:, cols], kv.at[0, my_rows, :], kv_sem.at[0, group], {"head": peer})
+        send(v_hbm.at[:, cols], kv.at[1, my_rows, :], kv_sem.at[1, group], {"head": peer})
     for n, peer in enumerate(peers):
         cols = pl.ds(pl.multiple_of(peer * HEADS * SIZE, HEADS * SIZE), HEADS * SIZE)
         send(q_hbm.at[:, cols], q_in.at[my_rows, :], q_sem.at[group], {"head": peer})
@@ -146,19 +136,19 @@
 
     order = [(n + x * (CHUNKS // 2)) % CHUNKS for n in range(CHUNKS)]
 
-    def chunk_rows(c):
-        return pl.ds(pl.multiple_of(c * CHUNK, CHUNK), CHUNK)
+    def part_of(tile, c):
+        return kv.at[:, pl.ds(pl.multiple_of(tile * TOKENS + c * CHUNK, CHUNK), CHUNK), :]
 
     def to_next(c):
         return pltpu.make_async_remote_copy(
-            src_ref=kv.at[0, :, chunk_rows(c), :], dst_ref=kv.at[2, :, chunk_rows(c), :],
+            src_ref=part_of(0, c), dst_ref=part_of(2, c),
             send_sem=send_sem.at[32 + c], recv_sem=gap_sem.at[1, c],
             device_id={"seq": segment + 2}, device_id_type=MESH,
         )
 
     def to_sibling(c, source):
         return pltpu.make_async_remote_copy(
-            src_ref=kv.at[source, :, chunk_rows(c), :], dst_ref=kv.at[1, :, chunk_rows(c), :],
+            src_ref=part_of(source, c), dst_ref=part_of(1, c),
             send_sem=send_sem.at[36 + c], recv_sem=gap_sem.at[0, c],
             device_id={"seq": sibling}, device_id_type=MESH,
         )
@@ -170,8 +160,8 @@
 
             @pl.when(group != r)
             def _():
-                wait_for(kv.at[0, 0, rows, :], kv_sem.at[0, r])
-                wait_for(kv.at[0, 1, rows, :], kv_sem.at[1, r])
+                wait_for(kv.at[0, rows, :], kv_sem.at[0, r])
+                wait_for(kv.at[1, rows, :], kv_sem.at[1, r])
 
         @pl.when(has_next & (edge_source == 0))
         def _():
@@ -185,7 +175,7 @@
 
         @pl.when(has_before)
         def _():
-            wait_for(kv.at[2, :, chunk_rows(c), :], gap_sem.at[1, c])
+            wait_for(part_of(2, c), gap_sem.at[1, c])
 
         @pl.when(has_before & (odd == 1))
         def _():
@@ -193,11 +183,11 @@
 
     @pl.when(segment < 2)
     def _():
-        kv[2] = jnp.zeros(kv.shape[1:], BF16)
+        kv[:, 2 * TOKENS :, :] = jnp.zeros((2, TOKENS, SIZE), BF16)
 
     @pl.when(segment == 0)
     def _():
-        kv[1] = jnp.zeros(kv.shape[1:], BF16)
+        kv[:, TOKENS : 2 * TOKENS, :] = jnp.zeros((2, TOKENS, SIZE), BF16)
 
     own_copies[2].wait()
     for r in range(PEERS):
@@ -212,33 +202,38 @@
     @pl.when(segment > 0)
     def _():
         for c in range(CHUNKS):
-            wait_for(kv.at[1, :, pl.ds(c * CHUNK, CHUNK), :], gap_sem.at[0, c])
-
-    for t in range(3):
-        for i in range(2):
-            kv_t[t, i] = kv[t, i].T
+            wait_for(part_of(1, c), gap_sem.at[0, c])
+
     for copy in own_copies[3:]:
         copy.wait()
+
+    v_t[...] = kv[1].T
 
     seen = ancestor_seen(parents_ref, segment)
     weight = mask_ref[...].astype(F32) / count_ref[0].astype(F32)
     causal = lax.broadcasted_iota(jnp.int32, (BLOCK, BLOCK), 0) <= lax.broadcasted_iota(
         jnp.int32, (BLOCK, BLOCK), 1
     )
+
+    def down(row):
+        return jnp.broadcast_to(row, (SIZE, BLOCK)).T
+
     for half in range(2):
         tok = slice(half * BLOCK, (half + 1) * BLOCK)
-        tiles = [(2, 0), (2, BLOCK), (1, 0), (1, BLOCK)] + [(0, r) for r in range(0, (half + 1) * BLOCK, BLOCK)]
+        own_keys = (half + 1) * BLOCK
+        blocks = list(range(TOKENS, 3 * TOKENS, BLOCK)) + list(range(0, own_keys, BLOCK))
         for h in range(HEADS):
             rows = slice(h * TOKENS + half * BLOCK, h * TOKENS + (half + 1) * BLOCK)
             cols = slice(h * SIZE, (h + 1) * SIZE)
             slot = h % 2
             query = stacked_q[rows, :]
             tops = [None, None, None]
-            for n, (t, r) in enumerate(tiles):
-                s = dot(kv[t, 0, r : r + BLOCK, :], query, transposed=True)
-                if t == 0 and r == half * BLOCK:
+            for n, r in enumerate(blocks):
+                s = dot(kv[0, r : r + BLOCK, :], query, right=1)
+                if r == half * BLOCK:
                     s = jnp.where(causal, s, NEGATIVE)
                 scores[slot, n] = s
+                t = r // TOKENS
                 top = jnp.max(s.reshape(BLOCK // 8, 8, BLOCK), axis=0)
                 tops[t] = top if tops[t] is None else jnp.maximum(tops[t], top)
             top = tops[0]
@@ -247,34 +242,35 @@
             top = jnp.max(top, axis=0, keepdims=True) * EXP_SCALE
             shifts = [top] + [jnp.where(seen[gap - 1], top, -NEGATIVE) for gap in (1, 2)]
             total, out = None, None
-            for n, (t, r) in enumerate(tiles):
-                e = jnp.exp2(scores[slot, n] * EXP_SCALE - shifts[t])
+            for n, r in enumerate(blocks):
+                e = jnp.exp2(scores[slot, n] * EXP_SCALE - shifts[r // TOKENS])
                 part = jnp.sum(e.reshape(BLOCK // 8, 8, BLOCK), axis=0)
                 total = part if total is None else total + part
                 e = e.astype(BF16)
-                probs[t, r : r + BLOCK, rows] = e
-                o = dot(kv_t[t, 1, :, r : r + BLOCK], e)
-                out = o if out is None else out + o
+                probs[r : r + BLOCK, rows] = e
+                part = dot(v_t[:, r : r + BLOCK], e)
+                out = part if out is None else out + part
             inverse = 1.0 / jnp.sum(total, axis=0, keepdims=True)
             out = (out * inverse).T.astype(BF16)
             att[tok, cols] = out
-            factor = jnp.broadcast_to(weight[0:1, tok] * inverse, (SIZE, BLOCK)).T
-            g = (up[tok, cols].astype(F32) * factor).astype(BF16)
+            g = (up[tok, cols].astype(F32) * down(weight[0:1, tok] * inverse)).astype(BF16)
             stacked_g[rows, :] = g
             product = (g.astype(F32) * out.astype(F32)).T
             delta[0:1, rows] = jnp.sum(product, axis=0, keepdims=True)
 
-    def backward(t, half, first):
-        keys = slice(half * BLOCK, (half + 1) * BLOCK)
+    def score_gradient(start, stop, rows):
+        d = dot(kv[1, start:stop, :], stacked_g[rows, :], right=1)
+        d = probs[start:stop, rows].astype(F32) * (d - delta[0:1, rows])
+        dscore[start:stop, rows] = d.astype(BF16)
+
+    def ancestor_scores(t):
         for n in range(2 * HEADS):
-            rows = slice(n * BLOCK, (n + 1) * BLOCK)
-            d = dot(kv[t, 1, keys, :], stacked_g[rows, :], transposed=True)
-            d = (probs[t, keys, rows].astype(F32) * (d - delta[0:1, rows])).astype(BF16)
-            dscore[keys, rows] = d
-            part = dot(kv_t[t, 0, :, keys], d)
-            dq_t[:, rows] = part if first else dq_t[:, rows] + part
+            score_gradient(t * TOKENS, (t + 1) * TOKENS, slice(n * BLOCK, (n + 1) * BLOCK))
+
+    def ancestor_terms(t, half):
+        keys = slice(t * TOKENS + half * BLOCK, t * TOKENS + (half + 1) * BLOCK)
         ret_tx[t - 1, half, 0] = (dot(dscore[keys, :], stacked_q[...]) * SCALE).astype(BF16)
-        ret_tx[t - 1, half, 1] = dot(probs[t, keys, :], stacked_g[...]).astype(BF16)
+        ret_tx[t - 1, half, 1] = dot(probs[keys, :], stacked_g[...]).astype(BF16)
 
     def part_copy(half):
         return pltpu.make_async_remote_copy(
@@ -290,15 +286,17 @@
             device_id={"seq": segment - 2}, device_id_type=MESH,
         )
 
-    for half in range(2):
-        backward(2, half, half == 0)
+    ancestor_scores(2)
+    for half in range(2):
+        ancestor_terms(2, half)
 
         @pl.when((odd == 0) & has_before)
         def _():
             back_copy(half).start()
 
-    for half in range(2):
-        backward(1, half, False)
+    ancestor_scores(1)
+    for half in range(2):
+        ancestor_terms(1, half)
         part_copy(half).start()
 
     def join(half):
@@ -311,31 +309,32 @@
         def _():
             back_copy(half).start()
 
-    join(0)
-
-    for half in range(2):
-        seen_rows = (half + 1) * BLOCK
-        tok = slice(half * BLOCK, (half + 1) * BLOCK)
+    for half in range(2):
         for h in range(HEADS):
             rows = slice(h * TOKENS + half * BLOCK, h * TOKENS + (half + 1) * BLOCK)
-            d = dot(kv[0, 1, 0:seen_rows, :], stacked_g[rows, :], transposed=True)
-            d = (probs[0, 0:seen_rows, rows].astype(F32) * (d - delta[0:1, rows])).astype(BF16)
-            dscore[0:seen_rows, rows] = d
-            total = dq_t[:, rows] + dot(kv_t[0, 0, :, 0:seen_rows], d)
-            dq[tok, h * SIZE : (h + 1) * SIZE] = (total * SCALE).T.astype(BF16)
-        if half == 0:
-            join(1)
+            score_gradient(0, (half + 1) * BLOCK, rows)
     own_grad[0, 0:BLOCK] = dot(dscore[0:BLOCK, :], stacked_q[...]) * SCALE
-    own_grad[1, 0:BLOCK] = dot(probs[0, 0:BLOCK, :], stacked_g[...])
+    own_grad[1, 0:BLOCK] = dot(probs[0:BLOCK, :], stacked_g[...])
+    join(0)
     dk, dv = None, None
     for h in range(HEADS):
         rows = slice(h * TOKENS + BLOCK, (h + 1) * TOKENS)
-        a = dot(dscore[BLOCK:, rows], stacked_q[rows, :])
-        b = dot(probs[0, BLOCK:, rows], stacked_g[rows, :])
+        a = dot(dscore[BLOCK:TOKENS, rows], stacked_q[rows, :])
+        b = dot(probs[BLOCK:TOKENS, rows], stacked_g[rows, :])
         dk = a if dk is None else dk + a
         dv = b if dv is None else dv + b
     own_grad[0, BLOCK:] = dk * SCALE
     own_grad[1, BLOCK:] = dv
+    join(1)
+    for half in range(2):
+        own_keys = (half + 1) * BLOCK
+        for h in range(HEADS):
+            rows = slice(h * TOKENS + half * BLOCK, h * TOKENS + (half + 1) * BLOCK)
+            total = dot(dscore[TOKENS:, rows], kv[0, TOKENS:, :], left=0) + dot(
+                dscore[0:own_keys, rows], kv[0, 0:own_keys, :], left=0
+            )
+            tok = slice(half * BLOCK, (half + 1) * BLOCK)
+            dq[tok, h * SIZE : (h + 1) * SIZE] = (total * SCALE).astype(BF16)
 
     @pl.when(odd == 0)
     def _():
@@ -409,16 +408,15 @@
         out_specs=[vmem] * 4,
         scratch_shapes=[
             pltpu.VMEM((TOKENS, HEADS * SIZE), BF16),
-            pltpu.VMEM((3, 2, TOKENS, SIZE), BF16),
+            pltpu.VMEM((2, 3 * TOKENS, SIZE), BF16),
             pltpu.VMEM((TOKENS, HEADS * SIZE), BF16),
             pltpu.VMEM((rows, SIZE), BF16),
             pltpu.VMEM((rows, SIZE), BF16),
-            pltpu.VMEM((3, 2, SIZE, TOKENS), BF16),
-            pltpu.VMEM((3, TOKENS, rows), BF16),
+            pltpu.VMEM((SIZE, 3 * TOKENS), BF16),
+            pltpu.VMEM((3 * TOKENS, rows), BF16),
             pltpu.VMEM((2, 6, BLOCK, BLOCK), F32),
             pltpu.VMEM((8, rows), F32),
-            pltpu.VMEM((SIZE, rows), F32),
-            pltpu.VMEM((TOKENS, rows), BF16),
+            pltpu.VMEM((3 * TOKENS, rows), BF16),
             pltpu.VMEM((2, 2, 2, BLOCK, SIZE), BF16),
             pltpu.VMEM((2, 2, 2, BLOCK, SIZE), BF16),
             pltpu.VMEM((2, TOKENS, SIZE), F32),

time: 53.4 us -> 40.7 us (0.76)
  Pallas kernels: 51.8 us -> 39.3 us
    pallas_call x1, Pallas kernels: 50.7 us -> 38.2 us  [per_device(): pl.pallas_call(kernel, out_shape=[pltpu.VMEM(shape, BF16) for shape in sh...]
where the time goes in v3:
time: 40.7 us; the launch traced here: 40.6 us
  Pallas kernels  39.3 us (97%)
  between operations  1.29 us (3%)
    pallas_call x1, Pallas kernels, per_device(): pl.pallas_call(kernel, out_shape=[pltpu.VMEM(shape, BF16) for shape in sh...  38.2 us
    pallas_call x1, Pallas kernels, per_device(): pl.pallas_call(deliver, out_shape=[jax.ShapeDtypeStruct(shape, BF16) for...  1.08 us

profile of v3, /device:TPU:31, one launch (start us, length us, event | category | flops | bytes accessed | tf_op | source)
XLA Modules:
  0.0 40.6 jit_solution(12407261272919604225)
XLA Ops:
  1.3 38.2 %shard_map.102 = (bf16[512,512]{1,0:T(8,128)(2,1)S(1)}, bf16[512,512]{1,0:T(8,128)(2,1)S(1)}, bf16[512,128]{1,0:T(8,128)(2,1)S(1)}, bf16[512,128]{1,0:T(8,128)(2,1)S(1)}) custom-call(bf16[64,4096]{1,0:T(8,128)(2,1)} %q_hbm.1, bf16[64,1024]{1,0:T(8,128)(2,1)} %k_hbm.1, bf16[64,1024]{1,0:T(8,128)(2,1)} %v_hbm.1, bf16[512,512]{1,0:T(8,128)(2,1)} %up_hbm.1, ...), custom_call_target="tpu_custom_call" | custom-call | flops 5000000000 | bytes 3000000 | tf_op jit(solution)/shard_map/pallas_call | solution.py:404
  39.5 1.1 %shard_map.103 = (bf16[512,512]{1,0:T(8,128)(2,1)}, bf16[512,512]{1,0:T(8,128)(2,1)}, bf16[512,128]{1,0:T(8,128)(2,1)}, bf16[512,128]{1,0:T(8,128)(2,1)}) custom-call(bf16[512,512]{1,0:T(8,128)(2,1)S(1)} %get-tuple-element.8.refs_0_, bf16[512,512]{1,0:T(8,128)(2,1)S(1)} %get-tuple-element.9.refs_1_, bf16[512,128]{1,0:T(8,128)(2,1)S(1)} %get-tuple-element.10.refs_2_, ...), custom_call_target="tpu_custom_call" | custom-call | tf_op jit(solution)/shard_map/pallas_call | solution.py:438

commit v4 on v3

--- a/solution.py
+++ b/solution.py
@@ -20,6 +20,9 @@
 SCALE = 1.0 / math.sqrt(SIZE)
 EXP_SCALE = math.log2(math.e) * SCALE
 NEGATIVE = -1e30
+SLOTS = 8
+AHEAD_OWN = 8
+AHEAD_GAP = 1
 MESH = pl.DeviceIdType.MESH
 STEPS = [(1, 0), (1, 1), (1, 3), (1, 2), (0, 1), (0, 3), (0, 2)]
 
@@ -42,7 +45,7 @@
 def kernel(
     q_hbm, k_hbm, v_hbm, up_hbm, mask_hbm, parents_hbm, count_ref,
     att, dq, dk_out, dv_out,
-    q_in, kv, up, stacked_q, stacked_g, v_t, probs, scores, delta, dscore,
+    q_in, kv, up, stacked_q, stacked_g, v_t, own_sum, stats, probs, scores, delta, dscore,
     ret_tx, ret_rx, own_grad, mask_ref, parents_ref,
     kv_sem, q_sem, gap_sem, ret_sem, send_sem, edge_sem, local_sem,
 ):
@@ -171,15 +174,16 @@
         def _():
             to_sibling(c, 0).start()
 
-    for c in order:
-
-        @pl.when(has_before)
-        def _():
-            wait_for(part_of(2, c), gap_sem.at[1, c])
-
-        @pl.when(has_before & (odd == 1))
-        def _():
-            to_sibling(c, 2).start()
+    def from_before():
+        for c in order:
+
+            @pl.when(has_before)
+            def _():
+                wait_for(part_of(2, c), gap_sem.at[1, c])
+
+            @pl.when(has_before & (odd == 1))
+            def _():
+                to_sibling(c, 2).start()
 
     @pl.when(segment < 2)
     def _():
@@ -199,76 +203,134 @@
     for h in range(HEADS):
         stacked_q[h * TOKENS : (h + 1) * TOKENS, :] = q_in[:, h * SIZE : (h + 1) * SIZE]
 
-    @pl.when(segment > 0)
-    def _():
-        for c in range(CHUNKS):
-            wait_for(part_of(1, c), gap_sem.at[0, c])
-
     for copy in own_copies[3:]:
         copy.wait()
 
-    v_t[...] = kv[1].T
-
-    seen = ancestor_seen(parents_ref, segment)
-    weight = mask_ref[...].astype(F32) / count_ref[0].astype(F32)
+    @pl.when(edge_target == 0)
+    def _():
+        from_before()
+
     causal = lax.broadcasted_iota(jnp.int32, (BLOCK, BLOCK), 0) <= lax.broadcasted_iota(
         jnp.int32, (BLOCK, BLOCK), 1
     )
 
+    def column_max(s):
+        return jnp.max(s.reshape(BLOCK // 8, 8, BLOCK), axis=0)
+
+    def exponentials(slot, n, r, shift, rows, total, out):
+        e = jnp.exp2(scores[slot, n] * EXP_SCALE - shift)
+        part = jnp.sum(e.reshape(BLOCK // 8, 8, BLOCK), axis=0)
+        total = part if total is None else total + part
+        e = e.astype(BF16)
+        probs[r : r + BLOCK, rows] = e
+        part = dot(v_t[:, r : r + BLOCK], e)
+        return total, part if out is None else out + part
+
+    v_t[:, 0:TOKENS] = kv[1, 0:TOKENS, :].T
+    def pipelined(first, second, ahead):
+        steps = [(half, h) for half in range(2) for h in range(HEADS)]
+        results = []
+        for n in range(len(steps) + ahead):
+            if n < len(steps):
+                results.append(first(n % SLOTS, *steps[n]))
+            if n >= ahead:
+                second((n - ahead) % SLOTS, *steps[n - ahead], results[n - ahead])
+
+    def block_rows(half, h):
+        return slice(h * TOKENS + half * BLOCK, h * TOKENS + (half + 1) * BLOCK)
+
+    def own_scores(slot, half, h):
+        rows = block_rows(half, h)
+        top = None
+        for n in range(half + 1):
+            s = dot(kv[0, n * BLOCK : (n + 1) * BLOCK, :], stacked_q[rows, :], right=1)
+            if n == half:
+                s = jnp.where(causal, s, NEGATIVE)
+            scores[slot, n] = s
+            top = column_max(s) if top is None else jnp.maximum(top, column_max(s))
+        return jnp.ceil(jnp.max(top, axis=0, keepdims=True) * EXP_SCALE)
+
+    def own_exponentials(slot, half, h, top):
+        rows = block_rows(half, h)
+        total, out = None, None
+        for n in range(half + 1):
+            total, out = exponentials(slot, n, n * BLOCK, top, rows, total, out)
+        stats[0:1, rows] = top
+        stats[1:2, rows] = jnp.sum(total, axis=0, keepdims=True)
+        own_sum[:, rows] = out
+
+    pipelined(own_scores, own_exponentials, AHEAD_OWN)
+
+    @pl.when(edge_target == 1)
+    def _():
+        from_before()
+
+    @pl.when(segment > 0)
+    def _():
+        for c in range(CHUNKS):
+            wait_for(part_of(1, c), gap_sem.at[0, c])
+
+    seen = ancestor_seen(parents_ref, segment)
+    weight = mask_ref[...].astype(F32) / count_ref[0].astype(F32)
+
     def down(row):
         return jnp.broadcast_to(row, (SIZE, BLOCK)).T
 
-    for half in range(2):
+    v_t[:, TOKENS:] = kv[1, TOKENS:, :].T
+    blocks = list(range(TOKENS, 3 * TOKENS, BLOCK))
+
+    def gap_scores(slot, half, h):
+        tops = [None, None, None]
+        for n, r in enumerate(blocks):
+            s = dot(kv[0, r : r + BLOCK, :], stacked_q[block_rows(half, h), :], right=1)
+            scores[slot, n] = s
+            t = r // TOKENS
+            tops[t] = column_max(s) if tops[t] is None else jnp.maximum(tops[t], column_max(s))
+        top = jnp.maximum(*(jnp.where(seen[gap - 1], tops[gap], NEGATIVE) for gap in (1, 2)))
+        return jnp.ceil(jnp.max(top, axis=0, keepdims=True) * EXP_SCALE)
+
+    def gap_exponentials(slot, half, h, top):
+        rows = block_rows(half, h)
         tok = slice(half * BLOCK, (half + 1) * BLOCK)
-        own_keys = (half + 1) * BLOCK
-        blocks = list(range(TOKENS, 3 * TOKENS, BLOCK)) + list(range(0, own_keys, BLOCK))
+        cols = slice(h * SIZE, (h + 1) * SIZE)
+        own_top = stats[0:1, rows]
+        top = jnp.maximum(top, own_top)
+        shifts = [None] + [jnp.where(seen[gap - 1], top, -NEGATIVE) for gap in (1, 2)]
+        total, out = None, None
+        for n, r in enumerate(blocks):
+            total, out = exponentials(slot, n, r, shifts[r // TOKENS], rows, total, out)
+        alpha = jnp.exp2(own_top - top)
+        stats[2:3, rows] = alpha
+        inverse = 1.0 / (jnp.sum(total, axis=0, keepdims=True) + alpha * stats[1:2, rows])
+        out = ((out + alpha * own_sum[:, rows]) * inverse).T.astype(BF16)
+        att[tok, cols] = out
+        g = (up[tok, cols].astype(F32) * down(weight[0:1, tok] * inverse)).astype(BF16)
+        stacked_g[rows, :] = g
+        product = (g.astype(F32) * out.astype(F32)).T
+        delta[0:1, rows] = jnp.sum(product, axis=0, keepdims=True)
+
+    pipelined(gap_scores, gap_exponentials, AHEAD_GAP)
+
+    def score_gradient(start, stop, rows):
+        d = dot(kv[1, start:stop, :], stacked_g[rows, :], right=1) - delta[0:1, rows]
+        p = probs[start:stop, rows].astype(F32)
+        if start == 0:
+            p = p * stats[2:3, rows]
+            probs[start:stop, rows] = p.astype(BF16)
+        dscore[start:stop, rows] = (p * d).astype(BF16)
+
+    def ancestor_scores(t, half):
+        start = t * TOKENS + half * BLOCK
+        for n in range(2 * HEADS):
+            score_gradient(start, start + BLOCK, slice(n * BLOCK, (n + 1) * BLOCK))
+
+    def own_gradient(half):
         for h in range(HEADS):
-            rows = slice(h * TOKENS + half * BLOCK, h * TOKENS + (half + 1) * BLOCK)
-            cols = slice(h * SIZE, (h + 1) * SIZE)
-            slot = h % 2
-            query = stacked_q[rows, :]
-            tops = [None, None, None]
-            for n, r in enumerate(blocks):
-                s = dot(kv[0, r : r + BLOCK, :], query, right=1)
-                if r == half * BLOCK:
-                    s = jnp.where(causal, s, NEGATIVE)
-                scores[slot, n] = s
-                t = r // TOKENS
-                top = jnp.max(s.reshape(BLOCK // 8, 8, BLOCK), axis=0)
-                tops[t] = top if tops[t] is None else jnp.maximum(tops[t], top)
-            top = tops[0]
-            for gap in (1, 2):
-                top = jnp.maximum(top, jnp.where(seen[gap - 1], tops[gap], NEGATIVE))
-            top = jnp.max(top, axis=0, keepdims=True) * EXP_SCALE
-            shifts = [top] + [jnp.where(seen[gap - 1], top, -NEGATIVE) for gap in (1, 2)]
-            total, out = None, None
-            for n, r in enumerate(blocks):
-                e = jnp.exp2(scores[slot, n] * EXP_SCALE - shifts[r // TOKENS])
-                part = jnp.sum(e.reshape(BLOCK // 8, 8, BLOCK), axis=0)
-                total = part if total is None else total + part
-                e = e.astype(BF16)
-                probs[r : r + BLOCK, rows] = e
-                part = dot(v_t[:, r : r + BLOCK], e)
-                out = part if out is None else out + part
-            inverse = 1.0 / jnp.sum(total, axis=0, keepdims=True)
-            out = (out * inverse).T.astype(BF16)
-            att[tok, cols] = out
-            g = (up[tok, cols].astype(F32) * down(weight[0:1, tok] * inverse)).astype(BF16)
-            stacked_g[rows, :] = g
-            product = (g.astype(F32) * out.astype(F32)).T
-            delta[0:1, rows] = jnp.sum(product, axis=0, keepdims=True)
-
-    def score_gradient(start, stop, rows):
-        d = dot(kv[1, start:stop, :], stacked_g[rows, :], right=1)
-        d = probs[start:stop, rows].astype(F32) * (d - delta[0:1, rows])
-        dscore[start:stop, rows] = d.astype(BF16)
-
-    def ancestor_scores(t):
-        for n in range(2 * HEADS):
-            score_gradient(t * TOKENS, (t + 1) * TOKENS, slice(n * BLOCK, (n + 1) * BLOCK))
+            score_gradient(0, (half + 1) * BLOCK, block_rows(half, h))
 
     def ancestor_terms(t, half):
-        keys = slice(t * TOKENS + half * BLOCK, t * TOKENS + (half + 1) * BLOCK)
+        start = t * TOKENS + half * BLOCK
+        keys = slice(start, start + BLOCK)
         ret_tx[t - 1, half, 0] = (dot(dscore[keys, :], stacked_q[...]) * SCALE).astype(BF16)
         ret_tx[t - 1, half, 1] = dot(probs[keys, :], stacked_g[...]).astype(BF16)
 
@@ -286,16 +348,21 @@
             device_id={"seq": segment - 2}, device_id_type=MESH,
         )
 
-    ancestor_scores(2)
+    ancestor_scores(2, 0)
+    ancestor_scores(2, 1)
     for half in range(2):
+        if half == 1:
+            ancestor_scores(1, 0)
         ancestor_terms(2, half)
 
         @pl.when((odd == 0) & has_before)
         def _():
             back_copy(half).start()
 
-    ancestor_scores(1)
+    ancestor_scores(1, 1)
     for half in range(2):
+        if half == 1:
+            own_gradient(0)
         ancestor_terms(1, half)
         part_copy(half).start()
 
@@ -309,10 +376,7 @@
         def _():
             back_copy(half).start()
 
-    for half in range(2):
-        for h in range(HEADS):
-            rows = slice(h * TOKENS + half * BLOCK, h * TOKENS + (half + 1) * BLOCK)
-            score_gradient(0, (half + 1) * BLOCK, rows)
+    own_gradient(1)
     own_grad[0, 0:BLOCK] = dot(dscore[0:BLOCK, :], stacked_q[...]) * SCALE
     own_grad[1, 0:BLOCK] = dot(probs[0:BLOCK, :], stacked_g[...])
     join(0)
@@ -413,8 +477,10 @@
             pltpu.VMEM((rows, SIZE), BF16),
             pltpu.VMEM((rows, SIZE), BF16),
             pltpu.VMEM((SIZE, 3 * TOKENS), BF16),
+            pltpu.VMEM((SIZE, rows), F32),
+            pltpu.VMEM((8, rows), F32),
             pltpu.VMEM((3 * TOKENS, rows), BF16),
-            pltpu.VMEM((2, 6, BLOCK, BLOCK), F32),
+            pltpu.VMEM((SLOTS, 4, BLOCK, BLOCK), F32),
             pltpu.VMEM((8, rows), F32),
             pltpu.VMEM((3 * TOKENS, rows), BF16),
             pltpu.VMEM((2, 2, 2, BLOCK, SIZE), BF16),

time: 40.7 us -> 38.2 us (0.939)
  Pallas kernels: 39.3 us -> 36.7 us
    pallas_call x1, Pallas kernels: 38.2 us -> 35.7 us  [per_device(): pl.pallas_call(kernel, out_shape=[pltpu.VMEM(shape, BF16) for shape in sh...]
where the time goes in v4:
time: 38.2 us; the launch traced here: 38 us
  Pallas kernels  36.7 us (96%)
  between operations  1.29 us (3%)
    pallas_call x1, Pallas kernels, per_device(): pl.pallas_call(kernel, out_shape=[pltpu.VMEM(shape, BF16) for shape in sh...  35.7 us
    pallas_call x1, Pallas kernels, per_device(): pl.pallas_call(deliver, out_shape=[jax.ShapeDtypeStruct(shape, BF16) for...  1.08 us

profile of v4, /device:TPU:31, one launch (start us, length us, event | category | flops | bytes accessed | tf_op | source)
XLA Modules:
  0.0 38.0 jit_solution(963763009984356620)
XLA Ops:
  1.3 35.7 %shard_map.102 = (bf16[512,512]{1,0:T(8,128)(2,1)S(1)}, bf16[512,512]{1,0:T(8,128)(2,1)S(1)}, bf16[512,128]{1,0:T(8,128)(2,1)S(1)}, bf16[512,128]{1,0:T(8,128)(2,1)S(1)}) custom-call(bf16[64,4096]{1,0:T(8,128)(2,1)} %q_hbm.1, bf16[64,1024]{1,0:T(8,128)(2,1)} %k_hbm.1, bf16[64,1024]{1,0:T(8,128)(2,1)} %v_hbm.1, bf16[512,512]{1,0:T(8,128)(2,1)} %up_hbm.1, ...), custom_call_target="tpu_custom_call" | custom-call | flops 5000000000 | bytes 3000000 | tf_op jit(solution)/shard_map/pallas_call | solution.py:468
  36.9 1.1 %shard_map.103 = (bf16[512,512]{1,0:T(8,128)(2,1)}, bf16[512,512]{1,0:T(8,128)(2,1)}, bf16[512,128]{1,0:T(8,128)(2,1)}, bf16[512,128]{1,0:T(8,128)(2,1)}) custom-call(bf16[512,512]{1,0:T(8,128)(2,1)S(1)} %get-tuple-element.8.refs_0_, bf16[512,512]{1,0:T(8,128)(2,1)S(1)} %get-tuple-element.9.refs_1_, bf16[512,128]{1,0:T(8,128)(2,1)S(1)} %get-tuple-element.10.refs_2_, ...), custom_call_target="tpu_custom_call" | custom-call | tf_op jit(solution)/shard_map/pallas_call | solution.py:504
